TPU v7x, 512 devices: a whole 4x4x16 slice. The times are simulated.
512 devices in a mesh: group: 8 (over z_lo, core), seq: 64 (over y, x, z_hi).
Axes of the slice: x: 4, y: 4, z: 16 (z_hi: 4, z_lo: 4; z = z_hi * 4 + z_lo), core: 2. Of those that a mesh axis runs over, the one named last changes fastest.
Arguments:
- resp_queries: bfloat16 [8, 8192, 2048], P('group', 'seq'), may hold values from -30 to 30
- resp_keys: bfloat16 [8, 8192, 1024], P('group', 'seq'), may hold values from -6 to 6
- resp_values: bfloat16 [8, 8192, 1024], P('group', 'seq'), may hold values from -6 to 6
- grad_out: bfloat16 [8, 8192, 2048], P('group', 'seq'), may hold values from -6 to 6
- prompt_keys: bfloat16 [8, 128, 1024], P('group', 'seq'), may hold values from -6 to 6
- prompt_values: bfloat16 [8, 128, 1024], P('group', 'seq'), may hold values from -6 to 6
- rewards: float32 [8, 16], P('group'), may hold values from -4 to 4
- lengths: int32 [8, 16], P('group'), may hold values from 1 to 512, as said below
Outputs:
- query_grad: bfloat16 [8, 8192, 2048], P('group', 'seq')
- key_grad: bfloat16 [8, 8192, 1024], P('group', 'seq')
- value_grad: bfloat16 [8, 8192, 1024], P('group', 'seq')
- prompt_key_grad: bfloat16 [8, 128, 1024], P('group', 'seq')
- prompt_value_grad: bfloat16 [8, 128, 1024], P('group', 'seq')
Inputs may be any that keep to these rules, and one draw needn't show every extreme that they name: `lengths`: in every prompt one response has exactly 512 tokens.
All inputs are finite; a program needn't handle non-finite values.
Results may differ from a plain program's by a relative error of at most 0.022.
Values may be sent and summed in bfloat16 or wider, within the bound.
No kernel may reach another device: no remote copies, remote signals or barrier semaphores. Data moves between devices by JAX's collectives and lax.ppermute only.
A program may use at most 64 MiB of HBM per device.

v0:
```python
import jax
import jax.numpy as jnp
from jax import lax
from jax.sharding import PartitionSpec as P

HEAD_DIM = 128
RESP_DEVS = 4
RESP_MAX = 512


score_scale = 144.0 ** (-0.5)
logit_cap = 50.0


def shifted(value, axis, by):
    size = lax.axis_size(axis)
    pairs = [(i, i + by) for i in range(size) if 0 <= i + by < size]
    return lax.ppermute(value, axis, pairs)


def attend(queries, key_rows, value_rows, grad_rows, key_pos, query_pos):
    raw_score = (
        jnp.einsum("qgjd,kgd->qgjk", queries, key_rows, preferred_element_type=jnp.float32)
        * score_scale
    )
    capped = logit_cap * jnp.tanh(raw_score / logit_cap)
    visible = (key_pos[None, :] <= query_pos[:, None]) & (key_pos[None, :] >= 0)
    visible = visible[:, None, None, :]
    exp_score = jnp.where(visible, jnp.exp(capped), jnp.float32(0.0))
    attn_weight = exp_score / jnp.sum(exp_score, axis=-1, keepdims=True)
    weight_low = attn_weight.astype(jnp.bfloat16)
    output = jnp.einsum(
        "qgjk,kgd->qgjd", weight_low, value_rows, preferred_element_type=jnp.float32
    ).astype(jnp.bfloat16)
    row_delta = jnp.sum(
        grad_rows.astype(jnp.float32) * output.astype(jnp.float32), axis=-1, keepdims=True
    )
    grad_weight = jnp.einsum(
        "qgjd,kgd->qgjk", grad_rows, value_rows, preferred_element_type=jnp.float32
    )
    grad_score = (
        attn_weight * (grad_weight - row_delta) * (1.0 - (capped / logit_cap) ** 2) * score_scale
    ).astype(jnp.bfloat16)
    grad_query = jnp.einsum(
        "qgjk,kgd->qgjd", grad_score, key_rows, preferred_element_type=jnp.float32
    )
    grad_key = jnp.einsum("qgjk,qgjd->kgd", grad_score, queries, preferred_element_type=jnp.float32)
    grad_value = jnp.einsum(
        "qgjk,qgjd->kgd", weight_low, grad_rows, preferred_element_type=jnp.float32
    )
    return (grad_query, grad_key, grad_value)


def body(
    resp_queries, resp_keys, resp_values, grad_out, prompt_keys, prompt_values, rewards, lengths
):
    block_rows = resp_queries.shape[1]
    kv_width = resp_keys.shape[2]
    kv_count = kv_width // HEAD_DIM
    pair = resp_queries.shape[2] // kv_width
    seq_index = lax.axis_index("seq")
    block_place = seq_index % RESP_DEVS
    response_id = seq_index // RESP_DEVS
    resp_count = lengths.shape[1]
    count = lax.psum(jnp.sum(lengths.astype(jnp.float32)), "group")
    advantage = rewards[0] - jnp.mean(rewards[0])
    weight_all = advantage * jnp.float32(lax.axis_size("group") * resp_count * RESP_MAX) / count
    chosen = jnp.arange(resp_count, dtype=jnp.int32) == response_id
    tok_weight = jnp.sum(jnp.where(chosen, weight_all, jnp.float32(0.0)))
    resp_length = jnp.sum(jnp.where(chosen, lengths[0], 0))
    query_pos = block_place * block_rows + jnp.arange(block_rows, dtype=jnp.int32)
    scaled = jnp.where(query_pos < resp_length, tok_weight, jnp.float32(0.0))[:, None] * grad_out[
        0
    ].astype(jnp.float32)
    grad_rows = scaled.astype(jnp.bfloat16).reshape(block_rows, kv_count, pair, HEAD_DIM)
    queries = resp_queries[0].reshape(block_rows, kv_count, pair, HEAD_DIM)
    prompt_k, prompt_v = (
        lax.all_gather(prompt_keys[0], "seq", axis=0, tiled=True),
        lax.all_gather(prompt_values[0], "seq", axis=0, tiled=True),
    )
    prompt_all = prompt_k.shape[0]
    own_block = jnp.stack([resp_keys[0], resp_values[0]])
    earlier = [own_block]
    for distance in range(1, RESP_DEVS):
        earlier.append(shifted(own_block, "seq", distance))
    ordered = [earlier[RESP_DEVS - 1 - slot] for slot in range(RESP_DEVS)]
    all_keys = jnp.concatenate([prompt_k] + [block[0] for block in ordered], axis=0).reshape(
        -1, kv_count, HEAD_DIM
    )
    all_values = jnp.concatenate([prompt_v] + [block[1] for block in ordered], axis=0).reshape(
        -1, kv_count, HEAD_DIM
    )
    block_pos = [
        (block_place - (RESP_DEVS - 1 - slot)) * block_rows
        + jnp.arange(block_rows, dtype=jnp.int32)
        for slot in range(RESP_DEVS)
    ]
    key_pos = jnp.concatenate([jnp.zeros((prompt_all,), jnp.int32)] + block_pos)
    half_width = kv_count // 2
    query_parts, key_parts, value_parts = ([], [], [])
    for head_half in range(2):
        low_head = head_half * half_width
        high_head = low_head + half_width
        grad_query, grad_key, grad_value = attend(
            queries[:, low_head:high_head],
            all_keys[:, low_head:high_head],
            all_values[:, low_head:high_head],
            grad_rows[:, low_head:high_head],
            key_pos,
            query_pos,
        )
        query_parts.append(grad_query)
        key_parts.append(grad_key)
        value_parts.append(grad_value)
    grad_query = jnp.concatenate(query_parts, axis=1).reshape(
        block_rows, kv_count * pair * HEAD_DIM
    )
    grad_key = jnp.concatenate(key_parts, axis=1).reshape(-1, kv_width)
    grad_value = jnp.concatenate(value_parts, axis=1).reshape(-1, kv_width)
    terms = []
    for distance in range(RESP_DEVS):
        start = prompt_all + (RESP_DEVS - 1 - distance) * block_rows
        terms.append(
            jnp.stack(
                [grad_key[start : start + block_rows], grad_value[start : start + block_rows]]
            )
        )
    collected = terms[0]
    for distance in range(1, RESP_DEVS):
        collected = collected + shifted(
            terms[distance].astype(jnp.bfloat16), "seq", -distance
        ).astype(jnp.float32)
    prompt_key_sum, prompt_value_sum = (
        lax.psum_scatter(grad_key[:prompt_all], "seq", scatter_dimension=0, tiled=True),
        lax.psum_scatter(grad_value[:prompt_all], "seq", scatter_dimension=0, tiled=True),
    )
    return (
        grad_query.astype(jnp.bfloat16)[None],
        collected[0].astype(jnp.bfloat16)[None],
        collected[1].astype(jnp.bfloat16)[None],
        prompt_key_sum.astype(jnp.bfloat16)[None],
        prompt_value_sum.astype(jnp.bfloat16)[None],
    )


def solution(mesh):
    return jax.shard_map(
        body,
        mesh=mesh,
        in_specs=(
            P("group", "seq", None),
            P("group", "seq", None),
            P("group", "seq", None),
            P("group", "seq", None),
            P("group", "seq", None),
            P("group", "seq", None),
            P("group", None),
            P("group", None),
        ),
        out_specs=(
            P("group", "seq", None),
            P("group", "seq", None),
            P("group", "seq", None),
            P("group", "seq", None),
            P("group", "seq", None),
        ),
        check_vma=False,
    )
```

profile of v0, /device:TPU:32, one launch (start us, length us, event | category | flops | bytes accessed | tf_op | source)
XLA Modules:
  0.0 1109.8 jit_solution(3951017444092878786)
XLA Ops:
  0.7 1.2 copy.94
  1.8 1.1 copy.95
  3.8 9.9 collective-permute-start.2
  13.7 10.0 collective-permute-start.1
  23.7 6.4 collective-permute-start
  30.8 81.8 %psum.7 = f32[]{:T(128)} all-reduce(f32[]{:T(128)} %convert_reduce_fusion), channel_id=1, replica_groups=mesh['group'=8,'seq'=64] {'group'}, use_global_device_ids=true, to_apply=%region_4.5 | all-reduce | flops 1 | bytes 8 | tf_op jit(solution)/shard_map/psum | solution.py:65
  115.1 1.3 fusion.42
  116.4 1.3 compare_select_fusion
  119.0 224.1 %all-gather.1 = bf16[1,128,1024]{2,0,1:T(2,128)(2,1)S(1)} all-gather(bf16[1,2,1024]{2,0,1:T(2,128)(2,1)S(1)} %copy.104), channel_id=3, replica_groups=mesh['group'=8,'seq'=64] {'seq'}, dimensions={1}, use_global_device_ids=true | all-gather | bytes 266240 | tf_op jit(solution)/shard_map/all_gather | solution.py:79
  343.1 231.3 %all-gather = bf16[1,128,1024]{2,0,1:T(2,128)(2,1)S(1)} all-gather(bf16[1,2,1024]{2,0,1:T(2,128)(2,1)S(1)} %copy.92), channel_id=2, replica_groups=mesh['group'=8,'seq'=64] {'seq'}, dimensions={1}, use_global_device_ids=true | all-gather | bytes 266240 | tf_op jit(solution)/shard_map/all_gather | solution.py:78
  577.4 1.3 dynamic-slice
  580.7 1.8 fusion.47
  582.7 1.1 copy.99
  583.8 1.9 fusion.48
  585.7 1.8 copy.108
  587.5 1.8 copy.98
  589.3 1.1 constant_dynamic-update-slice_fusion.3
  591.4 1.6 fusion.9
  593.0 1.5 fusion.13
  597.2 1.4 fusion.6
  599.6 1.4 fusion.3
  605.3 2.0 copy.143
  608.5 1.2 copy.139
  610.9 1.8 copy.137
  614.7 1.8 copy.140
  617.0 1.1 copy.138
  618.9 1.4 collective-permute-start.4
  621.2 1.3 collective-permute-start.5
  622.5 1.3 collective-permute-start.3
  623.8 481.7 %all-reduce.4 = (bf16[128,1024]{1,0:T(8,128)(2,1)}, bf16[128,1024]{1,0:T(8,128)(2,1)S(1)}) all-reduce(f32[128,1024]{1,0:T(8,128)S(1)} %copy-done.3, f32[128,1024]{1,0:T(8,128)S(1)} %copy.142), channel_id=4, replica_groups=mesh['group'=8,'seq'=64] {'seq'}, use_global_device_ids=true, to_apply=%region_9.10.clone | all-reduce | flops 262144 | bytes 1572864
  1105.5 1.3 fusion.39
  1107.5 1.5 fusion.26
  (100 shorter events, 25.9 us)
Async XLA Ops:
  0.6 29.5 %copy-start.14 = (s32[1,16]{1,0:T(1,128)S(1)}, s32[1,16]{1,0:T(1,128)}, u32[]{:S(2)}) copy-start(s32[1,16]{1,0:T(1,128)} %param.15) | copy-start | bytes 196
  0.6 112.6 %copy-start.7 = (bf16[1,128,2048]{2,1,0:T(8,128)(2,1)S(1)}, bf16[1,128,2048]{2,1,0:T(8,128)(2,1)}, u32[]{:S(2)}) copy-start(bf16[1,128,2048]{2,1,0:T(8,128)(2,1)} %param.11) | copy-start | bytes 1572868
  3.8 575.5 %collective-permute-start.2 = (bf16[2,128,1024]{1,2,0:T(8,128)(2,1)}, bf16[2,128,1024]{1,2,0:T(8,128)(2,1)}, u32[]{:S(2)}, u32[]{:S(2)}) collective-permute-start(bf16[2,128,1024]{1,2,0:T(8,128)(2,1)} %pad_maximum_fusion.2), channel_id=1, source_target_pairs={{0,1},{1,2},{2,3},{3,4},{4,5},{5,6},{6,7},{7,8},{8,9},{9,10},{10,1... | collective-permute-start | bytes 1572872 | tf_op jit(solution)/shard_map/ppermute | solution.py:18
  13.7 567.0 %collective-permute-start.1 = (bf16[2,128,1024]{1,2,0:T(8,128)(2,1)}, bf16[2,128,1024]{1,2,0:T(8,128)(2,1)}, u32[]{:S(2)}, u32[]{:S(2)}) collective-permute-start(bf16[2,128,1024]{1,2,0:T(8,128)(2,1)} %pad_maximum_fusion.2), channel_id=1, source_target_pairs={{0,2},{1,3},{2,4},{3,5},{4,6},{5,7},{6,8},{7,9},{8,10},{9,11},{10,... | collective-permute-start | bytes 1572872 | tf_op jit(solution)/shard_map/ppermute | solution.py:18
  23.7 560.1 %collective-permute-start = (bf16[2,128,1024]{1,2,0:T(8,128)(2,1)}, bf16[2,128,1024]{1,2,0:T(8,128)(2,1)}, u32[]{:S(2)}, u32[]{:S(2)}) collective-permute-start(bf16[2,128,1024]{1,2,0:T(8,128)(2,1)} %pad_maximum_fusion.2), channel_id=1, source_target_pairs={{0,3},{1,4},{2,5},{3,6},{4,7},{5,8},{6,9},{7,10},{8,11},{9,12},{10... | collective-permute-start | bytes 1572872 | tf_op jit(solution)/shard_map/ppermute | solution.py:18
  113.2 0.7 copy-start.13
  113.5 5.4 copy-start.11
  113.5 5.4 copy-start.12
  575.7 1.3 copy-start.8
  589.3 1.2 copy-start.4
  589.3 1.5 copy-start.10
  593.0 1.5 copy-start.9
  608.3 1.3 copy-start.2
  608.3 2.3 copy-start.1
  612.6 3.9 copy-start
  616.7 1.3 copy-start.5
  616.7 3.6 copy-start.6
  618.9 4.9 copy-start.3
  618.9 488.6 %collective-permute-start.4 = (bf16[2,128,1024]{2,1,0:T(8,128)(2,1)}, bf16[2,128,1024]{2,1,0:T(8,128)(2,1)}, u32[]{:S(2)}, u32[]{:S(2)}) collective-permute-start(bf16[2,128,1024]{2,1,0:T(8,128)(2,1)} %pad_maximum_fusion.5), channel_id=1, source_target_pairs={{2,0},{3,1},{4,2},{5,3},{6,4},{7,5},{8,6},{9,7},{10,8},{11,9},{12,... | collective-permute-start | bytes 1572872 | tf_op jit(solution)/shard_map/ppermute | solution.py:18
  621.2 486.3 %collective-permute-start.5 = (bf16[2,128,1024]{2,1,0:T(8,128)(2,1)}, bf16[2,128,1024]{2,1,0:T(8,128)(2,1)}, u32[]{:S(2)}, u32[]{:S(2)}) collective-permute-start(bf16[2,128,1024]{2,1,0:T(8,128)(2,1)} %pad_maximum_fusion.6), channel_id=1, source_target_pairs={{3,0},{4,1},{5,2},{6,3},{7,4},{8,5},{9,6},{10,7},{11,8},{12,9},{13... | collective-permute-start | bytes 1572872 | tf_op jit(solution)/shard_map/ppermute | solution.py:18
  622.5 484.9 %collective-permute-start.3 = (bf16[2,128,1024]{2,1,0:T(8,128)(2,1)S(1)}, bf16[2,128,1024]{2,1,0:T(8,128)(2,1)S(1)}, u32[]{:S(2)}, u32[]{:S(2)}) collective-permute-start(bf16[2,128,1024]{2,1,0:T(8,128)(2,1)S(1)} %pad_maximum_fusion.4), channel_id=1, source_target_pairs={{1,0},{2,1},{3,2},{4,3},{5,4},{6,5},{7,6},{8,7},{9,8},{10,9},{11,1... | collective-permute-start | bytes 1572872 | tf_op jit(solution)/shard_map/ppermute | solution.py:18
where the time goes:
time: 1110 us
  blocking collectives  1020 us (92%)
  local copies, waits for them, and re-layouts  34 us (3%)
  starting transfers between devices  30.3 us (3%)
  other arithmetic  14.3 us (1%)
    unnamed x1, blocking collectives  482 us
    all_gather x1, blocking collectives, body(): lax.all_gather(prompt_keys[0], 'seq', axis=0, tiled=True)  231 us
    all_gather x1, blocking collectives, body(): lax.all_gather(prompt_values[0], 'seq', axis=0, tiled=True)  224 us
    psum x1, blocking collectives, body(): count = lax.psum(jnp.sum(lengths.astype(jnp.float32)), 'group')  81.8 us
    ppermute x6, starting transfers between devices, shifted(): return lax.ppermute(value, axis, pairs)  30.3 us
  transfers between devices with their start and end apart: 6, of which 0 were waited for; matrix products, arithmetic and copies ran while one was open for 2% of the time, Pallas kernels for 0%

commit v1 on v0

v1 whole, which is shorter than its diff:
```python
import jax
import jax.numpy as jnp
from jax import lax
from jax.experimental import pallas as pl
from jax.experimental.pallas import tpu as pltpu
from jax.sharding import PartitionSpec as P

HEAD_DIM = 128
RESP_DEVS = 4
RESP_MAX = 512
CHUNKS = 2

SCORE_SCALE = 144.0 ** (-0.5)
LOGIT_CAP = 50.0
VMEM_BYTES = 48 * 1024 * 1024


def contract(left, right, left_dim, right_dim):
    return lax.dot_general(
        left, right, (((left_dim,), (right_dim,)), ((), ())), preferred_element_type=jnp.float32
    )


def pack_kernel(key_ref, value_ref, *packed):
    width = packed[0].shape[1] // 2
    for chunk, out in enumerate(packed):
        cols = slice(chunk * width, (chunk + 1) * width)
        out[:, :width] = key_ref[0, :, cols]
        out[:, width:] = value_ref[0, :, cols]


def pack(keys, values):
    _, rows, width = keys.shape
    out = jax.ShapeDtypeStruct((rows, 2 * width // CHUNKS), keys.dtype)
    return pl.pallas_call(
        pack_kernel,
        out_shape=[out] * CHUNKS,
        compiler_params=pltpu.CompilerParams(vmem_limit_bytes=VMEM_BYTES),
        name="pack",
    )(keys, values)


def attend_kernel(
    place_ref, weight_ref, query_ref, grad_ref, prompt_ref, own_ref, *rest
):
    far_refs = rest[: RESP_DEVS - 1]
    dquery_ref, dprompt_ref, down_ref = rest[RESP_DEVS - 1 : RESP_DEVS + 2]
    dfar_refs = rest[RESP_DEVS + 2 :]
    rows = own_ref.shape[0]
    width = own_ref.shape[1] // 2
    place, length = place_ref[0], place_ref[1]
    weight = weight_ref[0]
    pair = query_ref.shape[2] // width
    slot = place * rows + lax.broadcasted_iota(jnp.int32, (rows, 1), 0)
    row_weight = jnp.where(slot < length, weight, jnp.float32(0.0))
    prompt_rows = prompt_ref.shape[0]
    total_keys = prompt_rows + RESP_DEVS * rows
    key_index = lax.broadcasted_iota(jnp.int32, (pair * rows, total_keys), 1)
    row_index = lax.broadcasted_iota(jnp.int32, (pair * rows, total_keys), 0) % rows
    last_far = prompt_rows + rows * (1 + place)
    own_key = key_index - prompt_rows
    visible = (key_index < last_far) & ((own_key >= rows) | (own_key <= row_index))
    blocks = [prompt_ref, own_ref, *far_refs]
    for head in range(width // HEAD_DIM):
        kcols = slice(head * HEAD_DIM, (head + 1) * HEAD_DIM)
        vcols = slice(width + head * HEAD_DIM, width + (head + 1) * HEAD_DIM)
        keys = jnp.concatenate([block[:, kcols] for block in blocks], axis=0)
        values = jnp.concatenate([block[:, vcols] for block in blocks], axis=0)
        qcols = [
            slice((head * pair + i) * HEAD_DIM, (head * pair + i + 1) * HEAD_DIM)
            for i in range(pair)
        ]
        queries = jnp.concatenate([query_ref[0, :, cols] for cols in qcols], axis=0)
        grads = jnp.concatenate(
            [
                (row_weight * grad_ref[0, :, cols].astype(jnp.float32)).astype(jnp.bfloat16)
                for cols in qcols
            ],
            axis=0,
        )
        squashed = jnp.tanh(contract(queries, keys, 1, 1) * (SCORE_SCALE / LOGIT_CAP))
        exp_score = jnp.where(visible, jnp.exp(LOGIT_CAP * squashed), jnp.float32(0.0))
        attn = exp_score * (1.0 / jnp.sum(exp_score, axis=1, keepdims=True))
        attn_low = attn.astype(jnp.bfloat16)
        output = contract(attn_low, values, 1, 0).astype(jnp.bfloat16)
        delta = jnp.sum(
            grads.astype(jnp.float32) * output.astype(jnp.float32), axis=1, keepdims=True
        )
        grad_weight = contract(grads, values, 1, 1)
        grad_score = (
            attn * (grad_weight - delta) * (SCORE_SCALE - SCORE_SCALE * squashed * squashed)
        ).astype(jnp.bfloat16)
        dquery = contract(grad_score, keys, 1, 0).astype(jnp.bfloat16)
        for i, cols in enumerate(qcols):
            dquery_ref[:, cols] = dquery[i * rows : (i + 1) * rows]
        dkeys = contract(grad_score, queries, 0, 0)
        dvalues = contract(attn_low, grads, 0, 0)
        start = 0
        for out in (dprompt_ref, down_ref, *dfar_refs):
            stop = start + out.shape[0]
            out[:, kcols] = dkeys[start:stop].astype(out.dtype)
            out[:, vcols] = dvalues[start:stop].astype(out.dtype)
            start = stop


def attend_chunk(chunk, place, weight, queries, grads, prompt, own, far):
    rows, both = own.shape
    qwidth = queries.shape[2] // CHUNKS
    whole = lambda array: pl.BlockSpec(array.shape, lambda i: (0,) * array.ndim)
    column = pl.BlockSpec((1, rows, qwidth), lambda i: (0, 0, chunk))
    smem = pl.BlockSpec(memory_space=pltpu.SMEM)
    outs = [
        jax.ShapeDtypeStruct((rows, qwidth), jnp.bfloat16),
        jax.ShapeDtypeStruct(prompt.shape, jnp.bfloat16),
        jax.ShapeDtypeStruct(own.shape, jnp.float32),
    ] + [jax.ShapeDtypeStruct(own.shape, jnp.bfloat16) for _ in far]
    keys = prompt.shape[0] + RESP_DEVS * rows
    return pl.pallas_call(
        attend_kernel,
        grid=(1,),
        in_specs=[smem, smem, column, column, whole(prompt), whole(own)] + [whole(f) for f in far],
        out_specs=[whole(o) for o in outs],
        out_shape=outs,
        compiler_params=pltpu.CompilerParams(vmem_limit_bytes=VMEM_BYTES),
        cost_estimate=pl.CostEstimate(
            flops=0,
            bytes_accessed=0,
            transcendentals=0,
        ),
        name="attend",
    )(place, weight, queries, grads, prompt, own, *far)


def spread(value, axis, groups=None):
    size = len(groups[0]) if groups else lax.axis_size(axis)
    copies = jnp.broadcast_to(value[None], (size, *value.shape))
    return lax.all_to_all(copies, axis, 0, 0, axis_index_groups=groups)


def body(
    resp_queries, resp_keys, resp_values, grad_out, prompt_keys, prompt_values, rewards, lengths
):
    block_rows = resp_queries.shape[1]
    kv_width = resp_keys.shape[2]
    half = kv_width // CHUNKS
    seq_size = lax.axis_size("seq")
    resp_all = seq_size // RESP_DEVS
    seq_index = lax.axis_index("seq")
    place = seq_index % RESP_DEVS
    response_id = seq_index // RESP_DEVS
    resp_count = lengths.shape[1]
    along = [[r * RESP_DEVS + b for b in range(RESP_DEVS)] for r in range(resp_all)]
    across = [[r * RESP_DEVS + b for r in range(resp_all)] for b in range(RESP_DEVS)]

    def shifted(value, by):
        pairs = [
            (line[b], line[b + by])
            for line in along
            for b in range(RESP_DEVS)
            if 0 <= b + by < RESP_DEVS
        ]
        return lax.ppermute(value, "seq", pairs)

    own = pack(resp_keys, resp_values)
    far = [[shifted(own[c], d) for d in range(1, RESP_DEVS)] for c in range(CHUNKS)]

    prompt_own = jnp.concatenate([prompt_keys[0], prompt_values[0]], axis=1)
    rows_here = prompt_own.shape[0]
    prompt_line = spread(prompt_own, "seq", along).reshape(RESP_DEVS * rows_here, 2 * kv_width)
    prompt = spread(prompt_line, "seq", across).reshape(seq_size * rows_here, 2 * kv_width)

    group_count = jnp.sum(lengths.astype(jnp.float32)).reshape(1, 1)
    count = jnp.sum(spread(group_count, "group"))
    advantage = rewards[0] - jnp.mean(rewards[0])
    weight_all = advantage * jnp.float32(lax.axis_size("group") * resp_count * RESP_MAX) / count
    chosen = jnp.arange(resp_count, dtype=jnp.int32) == response_id
    weight = jnp.sum(jnp.where(chosen, weight_all, jnp.float32(0.0))).reshape(1)
    length = jnp.sum(jnp.where(chosen, lengths[0], 0))
    where_it_is = jnp.stack([place, length]).astype(jnp.int32)

    dquery, dprompt, down, back = [], [], [], []
    for c in range(CHUNKS):
        cols = slice(c * half, (c + 1) * half)
        prompt_chunk = jnp.concatenate(
            [prompt[:, cols], prompt[:, kv_width + c * half : kv_width + (c + 1) * half]], axis=1
        )
        outs = attend_chunk(
            c, where_it_is, weight, resp_queries, grad_out, prompt_chunk, own[c], far[c]
        )
        dquery.append(outs[0])
        dprompt.append(outs[1])
        down.append(outs[2])
        back.append([shifted(outs[2 + d], -d) for d in range(1, RESP_DEVS)])

    terms = jnp.concatenate(
        [t[:, :half] for t in dprompt] + [t[:, half:] for t in dprompt], axis=1
    )
    sent = terms.reshape(resp_all, RESP_DEVS * rows_here, 2 * kv_width)
    got = lax.all_to_all(sent, "seq", 0, 0, axis_index_groups=across)
    line_sum = jnp.sum(got.astype(jnp.float32), axis=0).astype(jnp.bfloat16)
    got = lax.all_to_all(
        line_sum.reshape(RESP_DEVS, rows_here, 2 * kv_width), "seq", 0, 0, axis_index_groups=along
    )
    prompt_sum = jnp.sum(got.astype(jnp.float32), axis=0).astype(jnp.bfloat16)

    total = [
        down[c] + sum(b.astype(jnp.float32) for b in back[c]) for c in range(CHUNKS)
    ]
    dkey = jnp.concatenate([t[:, :half].astype(jnp.bfloat16) for t in total], axis=1)
    dvalue = jnp.concatenate([t[:, half:].astype(jnp.bfloat16) for t in total], axis=1)
    return (
        jnp.concatenate(dquery, axis=1)[None],
        dkey[None],
        dvalue[None],
        prompt_sum[None, :, :kv_width],
        prompt_sum[None, :, kv_width:],
    )


def solution(mesh):
    split = P("group", "seq", None)
    return jax.shard_map(
        body,
        mesh=mesh,
        in_specs=(split,) * 6 + (P("group", None),) * 2,
        out_specs=(split,) * 5,
        check_vma=False,
    )
```

time: 1110 us -> 254 us (0.23)
  the two profiles are of different devices: /device:TPU:32 before, /device:TPU:98 now
where the time goes in v1:
time: 254 us; the launch traced here: 253 us
  waiting for transfers between devices  166 us (65%)
  starting transfers between devices  58.5 us (23%)
  Pallas kernels  10.4 us (4%)
  other arithmetic  10.2 us (4%)
  local copies, waits for them, and re-layouts  5.52 us (2%)
    ppermute x12, waiting for transfers between devices, shifted(): return lax.ppermute(value, 'seq', pairs)  140 us
    all_to_all x3, starting transfers between devices, spread(): return lax.all_to_all(copies, axis, 0, 0, axis_index_groups=groups)  25.3 us
    ppermute x12, starting transfers between devices, shifted(): return lax.ppermute(value, 'seq', pairs)  22.6 us
    all_to_all x3, waiting for transfers between devices, spread(): return lax.all_to_all(copies, axis, 0, 0, axis_index_groups=groups)  14.3 us
    all_to_all x1, waiting for transfers between devices, body(): lax.all_to_all(line_sum.reshape(RESP_DEVS, rows_here, 2 * kv_width), 'seq...  11.8 us
    pallas_call x2, Pallas kernels, attend_chunk(): pl.pallas_call(attend_kernel, grid=(1,), in_specs=[smem, smem, column, co...  10.4 us
    all_to_all x1, starting transfers between devices, body(): got = lax.all_to_all(sent, 'seq', 0, 0, axis_index_groups=across)  7.35 us
  transfers between devices with their start and end apart: 17, of which 10 were waited for; matrix products, arithmetic and copies ran while one was open for 3% of the time, Pallas kernels for 4%

profile of v1, /device:TPU:98, one launch (start us, length us, event | category | flops | bytes accessed | tf_op | source)
XLA Modules:
  0.0 252.6 jit_solution(17982090294919454798)
XLA Ops:
  2.0 12.5 %all-to-all-start.1 = ((bf16[4,2,2048]{2,1,0:T(2,128)(2,1)}), bf16[4,2,2048]{2,1,0:T(2,128)(2,1)S(1)}, u32[]{:S(2)}, u32[]{:S(2)}) async-start(bf16[4,2,2048]{2,1,0:T(2,128)(2,1)} %broadcast_in_dim.44), calls=%async_computation.1 | async-start | bytes 65536 | tf_op jit(solution)/shard_map/all_to_all | solution.py:137
  15.1 12.1 %all-to-all-done.1 = bf16[4,2,2048]{2,1,0:T(2,128)(2,1)S(1)} async-done(((bf16[4,2,2048]{2,1,0:T(2,128)(2,1)}), bf16[4,2,2048]{2,1,0:T(2,128)(2,1)S(1)}, u32[]{:S(2)}, u32[]{:S(2)}) %all-to-all-start.1) | async-done | bytes 32800 | tf_op jit(solution)/shard_map/all_to_all | solution.py:137
  27.3 1.2 broadcast_in_dim.42
  28.5 5.1 %all-to-all-start = ((f32[8,1,1]{2,1,0:T(1,128)}), f32[8,1,1]{2,1,0:T(1,128)S(1)}, u32[]{:S(2)}, u32[]{:S(2)}) async-start(f32[8,1,1]{2,1,0:T(1,128)} %broadcast_in_dim.42), calls=%async_computation | async-start | bytes 8192 | tf_op jit(solution)/shard_map/all_to_all | solution.py:137
  33.7 2.2 all-to-all-done
  36.7 7.6 %all-to-all-start.2 = ((bf16[16,8,2048]{2,1,0:T(8,128)(2,1)}), bf16[16,8,2048]{2,1,0:T(8,128)(2,1)S(1)}, u32[]{:S(2)}, u32[]{:S(2)}) async-start(bf16[16,8,2048]{2,1,0:T(8,128)(2,1)} %broadcast_in_dim.46), calls=%async_computation.2 | async-start | bytes 1048576 | tf_op jit(solution)/shard_map/all_to_all | solution.py:137
  44.4 2.4 collective-permute-start.2
  46.8 1.3 collective-permute-start.1
  48.1 1.3 collective-permute-start.5
  49.4 1.3 collective-permute-start.4
  50.7 7.2 %collective-permute-start.3 = (bf16[128,1024]{1,0:T(8,128)(2,1)S(1)}, bf16[128,1024]{1,0:T(8,128)(2,1)S(1)}, u32[]{:S(2)}, u32[]{:S(2)}) collective-permute-start(bf16[128,1024]{1,0:T(8,128)(2,1)S(1)} %get-tuple-element.21.own_ref), channel_id=1, source_target_pairs={{0,1},{1,2},{2,3},{4,5},{5,6},{6,7},{8,9},{9,10},{10,11},{12,13},{... | collective-permute-start | bytes 786440 | tf_op jit(solution)/shard_map/ppermute | solution.py:162
  61.9 1.2 fusion.1
  63.2 24.1 %collective-permute-done.5.rest_2_ = bf16[128,1024]{1,0:T(8,128)(2,1)S(1)} collective-permute-done((bf16[128,1024]{1,0:T(8,128)(2,1)S(1)}, bf16[128,1024]{1,0:T(8,128)(2,1)S(1)}, u32[]{:S(2)}, u32[]{:S(2)}) %collective-permute-start.5) | collective-permute-done | bytes 262176 | tf_op jit(solution)/shard_map/ppermute | solution.py:162
  87.3 1.3 collective-permute-start
  88.6 2.6 %collective-permute-done.4.rest_1_ = bf16[128,1024]{1,0:T(8,128)(2,1)S(1)} collective-permute-done((bf16[128,1024]{1,0:T(8,128)(2,1)S(1)}, bf16[128,1024]{1,0:T(8,128)(2,1)S(1)}, u32[]{:S(2)}, u32[]{:S(2)}) %collective-permute-start.4) | collective-permute-done | bytes 262176 | tf_op jit(solution)/shard_map/ppermute | solution.py:162
  91.2 2.5 collective-permute-done.3.rest_0_
  93.7 5.2 %attend.3 = (bf16[128,1024]{1,0:T(8,128)(2,1)S(1)}, bf16[128,1024]{1,0:T(8,128)(2,1)S(1)}, f32[128,1024]{1,0:T(8,128)S(1)}, bf16[128,1024]{1,0:T(8,128)(2,1)S(1)...) custom-call(s32[2]{0:T(128)S(1)} %pad_add_fusion.place_ref, f32[1]{0:T(128)} %bitcast.4.weight_ref, ...), custom_call_target="tpu_custom_call" | custom-call | tf_op jit(solution)/shard_map/attend/pallas_call | solution.py:118
  98.9 1.3 collective-permute-start.9
  100.2 1.3 collective-permute-start.10
  101.5 1.3 collective-permute-start.11
  102.8 5.2 %attend.2 = (bf16[128,1024]{1,0:T(8,128)(2,1)S(1)}, bf16[128,1024]{1,0:T(8,128)(2,1)S(1)}, f32[128,1024]{1,0:T(8,128)S(1)}, bf16[128,1024]{1,0:T(8,128)(2,1)S(1)...) custom-call(s32[2]{0:T(128)S(1)} %pad_add_fusion.place_ref, f32[1]{0:T(128)} %bitcast.4.weight_ref, ...), custom_call_target="tpu_custom_call" | custom-call | tf_op jit(solution)/shard_map/attend/pallas_call | solution.py:118
  109.7 7.3 %all-to-all-start.3 = ((bf16[16,8,2048]{2,1,0:T(8,128)(2,1)}), bf16[16,8,2048]{2,1,0:T(8,128)(2,1)}, u32[]{:S(2)}, u32[]{:S(2)}) async-start(bf16[16,8,2048]{2,1,0:T(8,128)(2,1)} %maximum_bitcast_fusion.1), calls=%async_computation.3 | async-start | bytes 1048576 | tf_op jit(solution)/shard_map/all_to_all | solution.py:199
  117.0 1.3 collective-permute-start.6
  118.3 1.3 collective-permute-start.7
  120.5 1.3 collective-permute-start.8
  121.8 8.3 %collective-permute-done.10 = bf16[128,1024]{1,0:T(8,128)(2,1)} collective-permute-done((bf16[128,1024]{1,0:T(8,128)(2,1)S(1)}, bf16[128,1024]{1,0:T(8,128)(2,1)}, u32[]{:S(2)}, u32[]{:S(2)}) %collective-permute-start.10) | collective-permute-done | bytes 262176 | tf_op jit(solution)/shard_map/ppermute | solution.py:162
  130.1 1.2 add_convert_fusion
  131.3 4.1 %collective-permute-done.6 = bf16[128,1024]{1,0:T(8,128)(2,1)S(1)} collective-permute-done((bf16[128,1024]{1,0:T(8,128)(2,1)S(1)}, bf16[128,1024]{1,0:T(8,128)(2,1)S(1)}, u32[]{:S(2)}, u32[]{:S(2)}) %collective-permute-start.6) | collective-permute-done | bytes 262176 | tf_op jit(solution)/shard_map/ppermute | solution.py:162
  135.5 11.6 %collective-permute-done.7 = bf16[128,1024]{1,0:T(8,128)(2,1)S(1)} collective-permute-done((bf16[128,1024]{1,0:T(8,128)(2,1)S(1)}, bf16[128,1024]{1,0:T(8,128)(2,1)S(1)}, u32[]{:S(2)}, u32[]{:S(2)}) %collective-permute-start.7) | collective-permute-done | bytes 262176 | tf_op jit(solution)/shard_map/ppermute | solution.py:162
  147.1 87.1 %collective-permute-done.8 = bf16[128,1024]{1,0:T(8,128)(2,1)S(1)} collective-permute-done((bf16[128,1024]{1,0:T(8,128)(2,1)S(1)}, bf16[128,1024]{1,0:T(8,128)(2,1)S(1)}, u32[]{:S(2)}, u32[]{:S(2)}) %collective-permute-start.8) | collective-permute-done | bytes 262176 | tf_op jit(solution)/shard_map/ppermute | solution.py:162
  236.1 3.3 %all-to-all-start.4 = ((bf16[4,2,2048]{2,1,0:T(2,128)(2,1)}), bf16[4,2,2048]{2,1,0:T(2,128)(2,1)S(1)}, u32[]{:S(2)}, u32[]{:S(2)}) async-start(bf16[4,2,2048]{2,1,0:T(2,128)(2,1)} %reshape.36), calls=%async_computation.4 | async-start | bytes 65536 | tf_op jit(solution)/shard_map/all_to_all | solution.py:201
  240.2 11.8 %all-to-all-done.4 = bf16[4,2,2048]{2,1,0:T(2,128)(2,1)S(1)} async-done(((bf16[4,2,2048]{2,1,0:T(2,128)(2,1)}), bf16[4,2,2048]{2,1,0:T(2,128)(2,1)S(1)}, u32[]{:S(2)}, u32[]{:S(2)}) %all-to-all-start.4) | async-done | bytes 32800 | tf_op jit(solution)/shard_map/all_to_all | solution.py:201
  (52 shorter events, 12.1 us)
Async XLA Ops:
  2.0 12.5 %copy-start.9 = (s32[1,16]{1,0:T(1,128)S(1)}, s32[1,16]{1,0:T(1,128)}, u32[]{:S(2)}) copy-start(s32[1,16]{1,0:T(1,128)} %param.15) | copy-start | bytes 196
  2.0 25.3 %all-to-all-start.1 = ((bf16[4,2,2048]{2,1,0:T(2,128)(2,1)}), bf16[4,2,2048]{2,1,0:T(2,128)(2,1)S(1)}, u32[]{:S(2)}, u32[]{:S(2)}) async-start(bf16[4,2,2048]{2,1,0:T(2,128)(2,1)} %broadcast_in_dim.44), calls=%async_computation.1 | async-start | bytes 65536 | tf_op jit(solution)/shard_map/all_to_all | solution.py:137
  28.5 7.4 %all-to-all-start = ((f32[8,1,1]{2,1,0:T(1,128)}), f32[8,1,1]{2,1,0:T(1,128)S(1)}, u32[]{:S(2)}, u32[]{:S(2)}) async-start(f32[8,1,1]{2,1,0:T(1,128)} %broadcast_in_dim.42), calls=%async_computation | async-start | bytes 8192 | tf_op jit(solution)/shard_map/all_to_all | solution.py:137
  36.7 7.6 %copy-start.2 = (bf16[1,128,1024]{2,1,0:T(8,128)(2,1)S(1)}, bf16[1,128,1024]{2,1,0:T(8,128)(2,1)}, u32[]{:S(2)}) copy-start(bf16[1,128,1024]{2,1,0:T(8,128)(2,1)} %key_ref.1) | copy-start | bytes 786436
  36.7 7.6 %copy-start.3 = (bf16[1,128,1024]{2,1,0:T(8,128)(2,1)S(1)}, bf16[1,128,1024]{2,1,0:T(8,128)(2,1)}, u32[]{:S(2)}) copy-start(bf16[1,128,1024]{2,1,0:T(8,128)(2,1)} %value_ref.1) | copy-start | bytes 786436
  36.7 26.4 %all-to-all-start.2 = ((bf16[16,8,2048]{2,1,0:T(8,128)(2,1)}), bf16[16,8,2048]{2,1,0:T(8,128)(2,1)S(1)}, u32[]{:S(2)}, u32[]{:S(2)}) async-start(bf16[16,8,2048]{2,1,0:T(8,128)(2,1)} %broadcast_in_dim.46), calls=%async_computation.2 | async-start | bytes 1048576 | tf_op jit(solution)/shard_map/all_to_all | solution.py:137
  44.4 57.2 %collective-permute-start.2 = (bf16[128,1024]{1,0:T(8,128)(2,1)S(1)}, bf16[128,1024]{1,0:T(8,128)(2,1)S(1)}, u32[]{:S(2)}, u32[]{:S(2)}) collective-permute-start(bf16[128,1024]{1,0:T(8,128)(2,1)S(1)} %get-tuple-element.19.own_ref), channel_id=1, source_target_pairs={{0,3},{4,7},{8,11},{12,15},{16,19},{20,23},{24,27},{28,31},{32,35}... | collective-permute-start | bytes 786440 | tf_op jit(solution)/shard_map/ppermute | solution.py:162
  46.8 56.1 %collective-permute-start.1 = (bf16[128,1024]{1,0:T(8,128)(2,1)S(1)}, bf16[128,1024]{1,0:T(8,128)(2,1)S(1)}, u32[]{:S(2)}, u32[]{:S(2)}) collective-permute-start(bf16[128,1024]{1,0:T(8,128)(2,1)S(1)} %get-tuple-element.19.own_ref), channel_id=1, source_target_pairs={{0,2},{1,3},{4,6},{5,7},{8,10},{9,11},{12,14},{13,15},{16,18},{17,... | collective-permute-start | bytes 786440 | tf_op jit(solution)/shard_map/ppermute | solution.py:162
  48.1 39.2 %collective-permute-start.5 = (bf16[128,1024]{1,0:T(8,128)(2,1)S(1)}, bf16[128,1024]{1,0:T(8,128)(2,1)S(1)}, u32[]{:S(2)}, u32[]{:S(2)}) collective-permute-start(bf16[128,1024]{1,0:T(8,128)(2,1)S(1)} %get-tuple-element.21.own_ref), channel_id=1, source_target_pairs={{0,3},{4,7},{8,11},{12,15},{16,19},{20,23},{24,27},{28,31},{32,35}... | collective-permute-start | bytes 786440 | tf_op jit(solution)/shard_map/ppermute | solution.py:162
  49.4 41.8 %collective-permute-start.4 = (bf16[128,1024]{1,0:T(8,128)(2,1)S(1)}, bf16[128,1024]{1,0:T(8,128)(2,1)S(1)}, u32[]{:S(2)}, u32[]{:S(2)}) collective-permute-start(bf16[128,1024]{1,0:T(8,128)(2,1)S(1)} %get-tuple-element.21.own_ref), channel_id=1, source_target_pairs={{0,2},{1,3},{4,6},{5,7},{8,10},{9,11},{12,14},{13,15},{16,18},{17,... | collective-permute-start | bytes 786440 | tf_op jit(solution)/shard_map/ppermute | solution.py:162
  50.7 42.9 %collective-permute-start.3 = (bf16[128,1024]{1,0:T(8,128)(2,1)S(1)}, bf16[128,1024]{1,0:T(8,128)(2,1)S(1)}, u32[]{:S(2)}, u32[]{:S(2)}) collective-permute-start(bf16[128,1024]{1,0:T(8,128)(2,1)S(1)} %get-tuple-element.21.own_ref), channel_id=1, source_target_pairs={{0,1},{1,2},{2,3},{4,5},{5,6},{6,7},{8,9},{9,10},{10,11},{12,13},{... | collective-permute-start | bytes 786440 | tf_op jit(solution)/shard_map/ppermute | solution.py:162
  58.0 0.7 copy-start.8
  63.1 30.5 %copy-start.1 = (bf16[1,128,2048]{2,1,0:T(8,128)(2,1)S(1)}, bf16[1,128,2048]{2,1,0:T(8,128)(2,1)}, u32[]{:S(2)}) copy-start(bf16[1,128,2048]{2,1,0:T(8,128)(2,1)} %grad_ref.3) | copy-start | bytes 1572868
  63.2 30.5 %copy-start = (bf16[1,128,2048]{2,1,0:T(8,128)(2,1)S(1)}, bf16[1,128,2048]{2,1,0:T(8,128)(2,1)}, u32[]{:S(2)}) copy-start(bf16[1,128,2048]{2,1,0:T(8,128)(2,1)} %query_ref.3) | copy-start | bytes 1572868
  87.3 15.5 %collective-permute-start = (bf16[128,1024]{1,0:T(8,128)(2,1)S(1)}, bf16[128,1024]{1,0:T(8,128)(2,1)S(1)}, u32[]{:S(2)}, u32[]{:S(2)}) collective-permute-start(bf16[128,1024]{1,0:T(8,128)(2,1)S(1)} %get-tuple-element.19.own_ref), channel_id=1, source_target_pairs={{0,1},{1,2},{2,3},{4,5},{5,6},{6,7},{8,9},{9,10},{10,11},{12,13},{... | collective-permute-start | bytes 786440 | tf_op jit(solution)/shard_map/ppermute | solution.py:162
  98.9 21.6 %collective-permute-start.9 = (bf16[128,1024]{1,0:T(8,128)(2,1)S(1)}, bf16[128,1024]{1,0:T(8,128)(2,1)}, u32[]{:S(2)}, u32[]{:S(2)}) collective-permute-start(bf16[128,1024]{1,0:T(8,128)(2,1)S(1)} %get-tuple-element.28), channel_id=1, source_target_pairs={{1,0},{2,1},{3,2},{5,4},{6,5},{7,6},{9,8},{10,9},{11,10},{13,12},{... | collective-permute-start | bytes 786440 | tf_op jit(solution)/shard_map/ppermute | solution.py:162
  100.2 29.9 %collective-permute-start.10 = (bf16[128,1024]{1,0:T(8,128)(2,1)S(1)}, bf16[128,1024]{1,0:T(8,128)(2,1)}, u32[]{:S(2)}, u32[]{:S(2)}) collective-permute-start(bf16[128,1024]{1,0:T(8,128)(2,1)S(1)} %get-tuple-element.29), channel_id=1, source_target_pairs={{2,0},{3,1},{6,4},{7,5},{10,8},{11,9},{14,12},{15,13},{18,16},{19,... | collective-permute-start | bytes 786440 | tf_op jit(solution)/shard_map/ppermute | solution.py:162
  101.5 28.5 %collective-permute-start.11 = (bf16[128,1024]{1,0:T(8,128)(2,1)S(1)}, bf16[128,1024]{1,0:T(8,128)(2,1)}, u32[]{:S(2)}, u32[]{:S(2)}) collective-permute-start(bf16[128,1024]{1,0:T(8,128)(2,1)S(1)} %get-tuple-element.30), channel_id=1, source_target_pairs={{3,0},{7,4},{11,8},{15,12},{19,16},{23,20},{27,24},{31,28},{35,32}... | collective-permute-start | bytes 786440 | tf_op jit(solution)/shard_map/ppermute | solution.py:162
  108.0 0.7 copy-start.4
  108.1 0.8 copy-start.6
  109.7 7.4 %copy-start.7 = (bf16[128,1024]{1,0:T(8,128)(2,1)S(1)}, bf16[128,1024]{1,0:T(8,128)(2,1)}, u32[]{:S(2)}) copy-start(bf16[128,1024]{1,0:T(8,128)(2,1)} %copy-done.6) | copy-start | bytes 786436
  109.7 8.7 %copy-start.5 = (bf16[128,1024]{1,0:T(8,128)(2,1)S(1)}, bf16[128,1024]{1,0:T(8,128)(2,1)}, u32[]{:S(2)}) copy-start(bf16[128,1024]{1,0:T(8,128)(2,1)} %copy-done.4) | copy-start | bytes 786436
  109.7 124.6 %all-to-all-start.3 = ((bf16[16,8,2048]{2,1,0:T(8,128)(2,1)}), bf16[16,8,2048]{2,1,0:T(8,128)(2,1)}, u32[]{:S(2)}, u32[]{:S(2)}) async-start(bf16[16,8,2048]{2,1,0:T(8,128)(2,1)} %maximum_bitcast_fusion.1), calls=%async_computation.3 | async-start | bytes 1048576 | tf_op jit(solution)/shard_map/all_to_all | solution.py:199
  117.0 18.4 %collective-permute-start.6 = (bf16[128,1024]{1,0:T(8,128)(2,1)S(1)}, bf16[128,1024]{1,0:T(8,128)(2,1)S(1)}, u32[]{:S(2)}, u32[]{:S(2)}) collective-permute-start(bf16[128,1024]{1,0:T(8,128)(2,1)S(1)} %copy-done.7), channel_id=1, source_target_pairs={{1,0},{2,1},{3,2},{5,4},{6,5},{7,6},{9,8},{10,9},{11,10},{13,12},{... | collective-permute-start | bytes 786440 | tf_op jit(solution)/shard_map/ppermute | solution.py:162
  118.3 28.7 %collective-permute-start.7 = (bf16[128,1024]{1,0:T(8,128)(2,1)S(1)}, bf16[128,1024]{1,0:T(8,128)(2,1)S(1)}, u32[]{:S(2)}, u32[]{:S(2)}) collective-permute-start(bf16[128,1024]{1,0:T(8,128)(2,1)S(1)} %copy-done.5), channel_id=1, source_target_pairs={{2,0},{3,1},{6,4},{7,5},{10,8},{11,9},{14,12},{15,13},{18,16},{19,... | collective-permute-start | bytes 786440 | tf_op jit(solution)/shard_map/ppermute | solution.py:162
  120.5 113.6 %collective-permute-start.8 = (bf16[128,1024]{1,0:T(8,128)(2,1)S(1)}, bf16[128,1024]{1,0:T(8,128)(2,1)S(1)}, u32[]{:S(2)}, u32[]{:S(2)}) collective-permute-start(bf16[128,1024]{1,0:T(8,128)(2,1)S(1)} %get-tuple-element.26), channel_id=1, source_target_pairs={{3,0},{7,4},{11,8},{15,12},{19,16},{23,20},{27,24},{31,28},{35,32}... | collective-permute-start | bytes 786440 | tf_op jit(solution)/shard_map/ppermute | solution.py:162
  236.1 15.9 %all-to-all-start.4 = ((bf16[4,2,2048]{2,1,0:T(2,128)(2,1)}), bf16[4,2,2048]{2,1,0:T(2,128)(2,1)S(1)}, u32[]{:S(2)}, u32[]{:S(2)}) async-start(bf16[4,2,2048]{2,1,0:T(2,128)(2,1)} %reshape.36), calls=%async_computation.4 | async-start | bytes 65536 | tf_op jit(solution)/shard_map/all_to_all | solution.py:201

commit v2 on v1

v2 whole, which is shorter than its diff:
```python
import jax
import jax.numpy as jnp
from jax import lax
from jax.experimental import pallas as pl
from jax.experimental.pallas import tpu as pltpu
from jax.sharding import PartitionSpec as P

HEAD_DIM = 128
RESP_DEVS = 4
RESP_MAX = 512
LOW_HEADS = 5

SCORE_SCALE = 144.0 ** (-0.5)
LOGIT_CAP = 50.0
VMEM_BYTES = 48 * 1024 * 1024
PARAMS = dict(compiler_params=pltpu.CompilerParams(vmem_limit_bytes=VMEM_BYTES))


def contract(left, right, left_dim, right_dim):
    return lax.dot_general(
        left, right, (((left_dim,), (right_dim,)), ((), ())), preferred_element_type=jnp.float32
    )


def pack_kernel(key_ref, value_ref, all_ref, low_ref, high_ref):
    low = low_ref.shape[2]
    for part, ref in enumerate((key_ref, value_ref)):
        all_ref[part] = ref[0]
        low_ref[part] = ref[0, :, :low]
        high_ref[part] = ref[0, :, low:]


def pack(keys, values):
    _, rows, width = keys.shape
    low = LOW_HEADS * HEAD_DIM
    return pl.pallas_call(
        pack_kernel,
        out_shape=[
            jax.ShapeDtypeStruct((2, rows, wide), keys.dtype) for wide in (width, low, width - low)
        ],
        name="pack",
        **PARAMS,
    )(keys, values)


def attend_kernel(place_ref, weight_ref, query_ref, grad_ref, prompt_key_ref, prompt_value_ref, own_ref, *rest):
    fars = rest[: RESP_DEVS - 1]
    dquery_ref, dprompt_key_ref, dprompt_value_ref, down_ref, *dfars = rest[-(RESP_DEVS + 3) :]
    rows = query_ref.shape[1]
    pair = query_ref.shape[2] // HEAD_DIM
    place, length = place_ref[0], place_ref[1]
    slot = place * rows + lax.broadcasted_iota(jnp.int32, (rows, 1), 0)
    row_weight = jnp.where(slot < length, weight_ref[0], jnp.float32(0.0))
    blocks = [own_ref, *fars]
    prompt_rows = prompt_key_ref.shape[0]
    total_keys = prompt_rows + RESP_DEVS * rows
    key_index = lax.broadcasted_iota(jnp.int32, (pair * rows, total_keys), 1)
    row_index = lax.broadcasted_iota(jnp.int32, (pair * rows, total_keys), 0) % rows
    last_far = prompt_rows + rows * (1 + place)
    own_key = key_index - prompt_rows
    visible = (key_index < last_far) & ((own_key >= rows) | (own_key <= row_index))
    keys = jnp.concatenate([prompt_key_ref[...]] + [block[0] for block in blocks], axis=0)
    values = jnp.concatenate([prompt_value_ref[...]] + [block[1] for block in blocks], axis=0)
    cols = [slice(i * HEAD_DIM, (i + 1) * HEAD_DIM) for i in range(pair)]
    queries = jnp.concatenate([query_ref[0, :, c] for c in cols], axis=0)
    grads = jnp.concatenate(
        [(row_weight * grad_ref[0, :, c].astype(jnp.float32)).astype(jnp.bfloat16) for c in cols],
        axis=0,
    )
    squashed = jnp.tanh(contract(queries, keys, 1, 1) * (SCORE_SCALE / LOGIT_CAP))
    exp_score = jnp.where(visible, jnp.exp(LOGIT_CAP * squashed), jnp.float32(0.0))
    attn = exp_score * (1.0 / jnp.sum(exp_score, axis=1, keepdims=True))
    attn_low = attn.astype(jnp.bfloat16)
    output = contract(attn_low, values, 1, 0).astype(jnp.bfloat16)
    delta = jnp.sum(grads.astype(jnp.float32) * output.astype(jnp.float32), axis=1, keepdims=True)
    grad_weight = contract(grads, values, 1, 1)
    grad_score = (
        attn * (grad_weight - delta) * (SCORE_SCALE - SCORE_SCALE * squashed * squashed)
    ).astype(jnp.bfloat16)
    dquery = contract(grad_score, keys, 1, 0).astype(jnp.bfloat16)
    for i, c in enumerate(cols):
        dquery_ref[0, :, c] = dquery[i * rows : (i + 1) * rows]
    dkeys = contract(grad_score, queries, 0, 0)
    dvalues = contract(attn_low, grads, 0, 0)
    dprompt_key_ref[...] = dkeys[:prompt_rows].astype(dprompt_key_ref.dtype)
    dprompt_value_ref[...] = dvalues[:prompt_rows].astype(dprompt_value_ref.dtype)
    start = prompt_rows
    for out in (down_ref, *dfars):
        stop = start + out.shape[1]
        out[0] = dkeys[start:stop].astype(out.dtype)
        out[1] = dvalues[start:stop].astype(out.dtype)
        start = stop


def attend_chunk(first, heads, where_it_is, weight, queries, grads, prompt, own, far, so_far):
    rows = queries.shape[1]
    all_heads = prompt.shape[1] // 2 // HEAD_DIM
    width = heads * HEAD_DIM
    qcols = queries.shape[2] // all_heads
    smem = pl.BlockSpec(memory_space=pltpu.SMEM)
    query_spec = pl.BlockSpec((1, rows, qcols), lambda i: (0, 0, first + i))
    prompt_block = (prompt.shape[0], HEAD_DIM)
    key_spec = pl.BlockSpec(prompt_block, lambda i: (0, first + i))
    value_spec = pl.BlockSpec(prompt_block, lambda i: (0, all_heads + first + i))
    own_spec = pl.BlockSpec((2, rows, HEAD_DIM), lambda i: (0, 0, i))
    held_specs = [
        pl.BlockSpec(
            (2, rows, HEAD_DIM),
            lambda i, base=first if held.shape[2] > width else 0: (0, 0, base + i),
        )
        for held in (own, *far)
    ]
    outs = [
        jax.ShapeDtypeStruct(queries.shape, jnp.bfloat16),
        jax.ShapeDtypeStruct((prompt.shape[0], all_heads * HEAD_DIM), jnp.bfloat16),
        jax.ShapeDtypeStruct((prompt.shape[0], all_heads * HEAD_DIM), jnp.bfloat16),
        jax.ShapeDtypeStruct((2, rows, width), jnp.float32),
    ] + [jax.ShapeDtypeStruct((2, rows, width), jnp.bfloat16) for _ in far]
    inputs = [where_it_is, weight, queries, grads, prompt, prompt, own, *far]
    specs = [smem, smem, query_spec, query_spec, key_spec, value_spec] + held_specs
    aliases = {len(inputs) + i: i for i in range(len(so_far))}
    return pl.pallas_call(
        attend_kernel,
        grid=(heads,),
        in_specs=specs + [pl.BlockSpec(memory_space=pl.ANY)] * len(so_far),
        out_specs=[query_spec, key_spec, key_spec] + [own_spec] * RESP_DEVS,
        out_shape=outs,
        input_output_aliases=aliases,
        cost_estimate=pl.CostEstimate(flops=0, bytes_accessed=0, transcendentals=0),
        name="attend",
        **PARAMS,
    )(*inputs, *so_far)


def finish_kernel(down_ref, *rest):
    backs = rest[:2]
    dkey_ref, dvalue_ref = rest[-2:]
    for part, out in enumerate((dkey_ref, dvalue_ref)):
        total = down_ref[part]
        for back in backs:
            total = total + back[part].astype(jnp.float32)
        out[0] = total.astype(out.dtype)


def finish_chunk(first, down, back, width, so_far):
    _, rows, _ = down.shape
    heads = down.shape[2] // HEAD_DIM
    spec = pl.BlockSpec((2, rows, HEAD_DIM), lambda i: (0, 0, i))
    out_spec = pl.BlockSpec((1, rows, HEAD_DIM), lambda i: (0, 0, first + i))
    inputs = [down, *back]
    return pl.pallas_call(
        finish_kernel,
        grid=(heads,),
        in_specs=[spec] * (1 + len(back))
        + [pl.BlockSpec(memory_space=pl.ANY)] * len(so_far),
        out_specs=[out_spec] * 2,
        out_shape=[jax.ShapeDtypeStruct((1, rows, width), jnp.bfloat16)] * 2,
        input_output_aliases={len(inputs) + i: i for i in range(len(so_far))},
        cost_estimate=pl.CostEstimate(flops=0, bytes_accessed=0, transcendentals=0),
        name="finish",
        **PARAMS,
    )(*inputs, *so_far)


def spread(value, axis, groups=None):
    size = len(groups[0]) if groups else lax.axis_size(axis)
    copies = jnp.broadcast_to(value[None], (size, *value.shape))
    return lax.all_to_all(copies, axis, 0, 0, axis_index_groups=groups)


def body(
    resp_queries, resp_keys, resp_values, grad_out, prompt_keys, prompt_values, rewards, lengths
):
    rows = resp_queries.shape[1]
    width = resp_keys.shape[2]
    seq_size = lax.axis_size("seq")
    resp_all = seq_size // RESP_DEVS
    seq_index = lax.axis_index("seq")
    place = seq_index % RESP_DEVS
    response_id = seq_index // RESP_DEVS
    resp_count = lengths.shape[1]
    prompt_part = prompt_keys.shape[1]
    along = [[r * RESP_DEVS + b for b in range(RESP_DEVS)] for r in range(resp_all)]
    across = [[r * RESP_DEVS + b for r in range(resp_all)] for b in range(RESP_DEVS)]

    def moved(value, *pairs):
        pairs = [(line[a], line[b]) for line in along for a, b in pairs]
        return lax.ppermute(value, "seq", pairs)

    own, own_low, own_high = pack(resp_keys, resp_values)
    low = own_low.shape[2]
    one = moved(own, (0, 1), (1, 2), (2, 3))
    low_three = moved(own_low, (0, 3), (1, 0))
    own_high, low_three = lax.optimization_barrier((own_high, low_three))
    low_two = moved(low_three, (0, 3), (3, 2))
    high_three = moved(own_high, (0, 3))
    high_two = moved(one[:, :, low:], (1, 2), (2, 3))

    prompt_own = jnp.concatenate([prompt_keys[0], prompt_values[0]], axis=1)
    prompt = spread(prompt_own, "seq", along).reshape(RESP_DEVS * prompt_part, 2 * width)
    prompt = spread(prompt, "seq", across).reshape(seq_size * prompt_part, 2 * width)

    group_count = jnp.sum(lengths.astype(jnp.float32)).reshape(1, 1)
    group_count, prompt = lax.optimization_barrier((group_count, prompt))
    count = jnp.sum(spread(group_count, "group"))
    advantage = rewards[0] - jnp.mean(rewards[0])
    advantage = advantage * jnp.float32(lax.axis_size("group") * resp_count * RESP_MAX) / count
    chosen = jnp.arange(resp_count, dtype=jnp.int32) == response_id
    weight = jnp.sum(jnp.where(chosen, advantage, jnp.float32(0.0))).reshape(1)
    length = jnp.sum(jnp.where(chosen, lengths[0], 0))
    where_it_is = jnp.stack([place, length]).astype(jnp.int32)

    fixed = where_it_is, weight, resp_queries, grad_out, prompt, own
    *so_far, down_low, b1, b2, b3 = attend_chunk(
        0, LOW_HEADS, *fixed, (one, low_two, low_three), []
    )
    low_passed = moved(b2, (2, 3), (3, 0))
    low_one = moved(b1, (3, 2), (2, 1), (1, 0))
    low_around = moved(b3 + low_passed, (3, 0), (0, 1))
    *so_far, down_high, b1, b2, b3 = attend_chunk(
        LOW_HEADS, width // HEAD_DIM - LOW_HEADS, *fixed, (one, high_two, high_three), so_far
    )
    high_passed = moved(b2, (3, 2), (2, 1))
    high_around = moved(b3, (3, 0))
    high_one = moved(b1 + high_passed, (3, 2), (2, 1), (1, 0))
    dquery, *dprompt = so_far
    terms = jnp.concatenate(dprompt, axis=1).reshape(resp_all, -1, 2 * width)
    terms, *_ = lax.optimization_barrier(
        (terms, low_one, low_passed, high_passed, high_around)
    )

    done = finish_chunk(0, down_low, (low_one, low_around), width, [])
    done = finish_chunk(LOW_HEADS, down_high, (high_one, high_around), width, done)

    got = lax.all_to_all(terms, "seq", 0, 0, axis_index_groups=across)
    line_sum = jnp.sum(got.astype(jnp.float32), axis=0)
    sent = line_sum.astype(jnp.bfloat16).reshape(RESP_DEVS, prompt_part, 2 * width)
    got = lax.all_to_all(sent, "seq", 0, 0, axis_index_groups=along)
    prompt_sum = jnp.sum(got.astype(jnp.float32), axis=0).astype(jnp.bfloat16)
    return (
        dquery,
        done[0],
        done[1],
        prompt_sum[None, :, :width],
        prompt_sum[None, :, width:],
    )


def solution(mesh):
    split = P("group", "seq", None)
    return jax.shard_map(
        body,
        mesh=mesh,
        in_specs=(split,) * 6 + (P("group", None),) * 2,
        out_specs=(split,) * 5,
        check_vma=False,
    )
```

time: 254 us -> 193 us (0.76)
  the two profiles are of different devices: /device:TPU:98 before, /device:TPU:2 now
where the time goes in v2:
time: 193 us; the launch traced here: 192 us
  starting transfers between devices  89.7 us (46%)
  waiting for transfers between devices  64.2 us (33%)
  Pallas kernels  17.6 us (9%)
  local copies, waits for them, and re-layouts  12.1 us (6%)
  other arithmetic  7.23 us (4%)
    ppermute x11, waiting for transfers between devices, moved(): return lax.ppermute(value, 'seq', pairs)  38.3 us
    ppermute x11, starting transfers between devices, moved(): return lax.ppermute(value, 'seq', pairs)  38.2 us
    all_to_all x3, starting transfers between devices, spread(): return lax.all_to_all(copies, axis, 0, 0, axis_index_groups=groups)  26 us
    all_to_all x1, starting transfers between devices, body(): got = lax.all_to_all(sent, 'seq', 0, 0, axis_index_groups=along)  18 us
    all_to_all x3, waiting for transfers between devices, spread(): return lax.all_to_all(copies, axis, 0, 0, axis_index_groups=groups)  16.7 us
    pallas_call x2, Pallas kernels, attend_chunk(): pl.pallas_call(attend_kernel, grid=(heads,), in_specs=specs + [pl.BlockSp...  14.1 us
    all_to_all x1, waiting for transfers between devices, body(): got = lax.all_to_all(sent, 'seq', 0, 0, axis_index_groups=along)  9.21 us
    all_to_all x1, starting transfers between devices, body(): got = lax.all_to_all(terms, 'seq', 0, 0, axis_index_groups=across)  7.48 us
  transfers between devices with their start and end apart: 16, of which 6 were waited for; matrix products, arithmetic and copies ran while one was open for 5% of the time, Pallas kernels for 9%

profile of v2, /device:TPU:2, one launch (start us, length us, event | category | flops | bytes accessed | tf_op | source)
XLA Modules:
  0.0 192.3 jit_solution(2644146242943603117)
XLA Ops:
  2.0 15.1 %all-to-all-start = ((bf16[4,2,2048]{2,1,0:T(2,128)(2,1)}), bf16[4,2,2048]{2,1,0:T(2,128)(2,1)S(1)}, u32[]{:S(2)}, u32[]{:S(2)}) async-start(bf16[4,2,2048]{2,1,0:T(2,128)(2,1)} %broadcast_in_dim.36), calls=%async_computation | async-start | bytes 65536 | tf_op jit(solution)/shard_map/all_to_all | solution.py:168
  17.1 0.9 copy-done.12
  18.0 0.9 copy-done.13
  19.7 7.8 %collective-permute-start.2 = (bf16[2,128,640]{2,1,0:T(8,128)(2,1)S(1)}, bf16[2,128,640]{2,1,0:T(8,128)(2,1)S(1)}, u32[]{:S(2)}, u32[]{:S(2)}) collective-permute-start(bf16[2,128,640]{2,1,0:T(8,128)(2,1)S(1)} %get-tuple-element.35), channel_id=1, source_target_pairs={{0,3},{1,0},{4,7},{5,4},{8,11},{9,8},{12,15},{13,12},{16,19},{17,1... | collective-permute-start | bytes 983048 | tf_op jit(solution)/shard_map/ppermute | solution.py:188
  27.6 2.0 %collective-permute-start = (bf16[2,128,1024]{2,1,0:T(8,128)(2,1)S(1)}, bf16[2,128,1024]{2,1,0:T(8,128)(2,1)S(1)}, u32[]{:S(2)}, u32[]{:S(2)}) collective-permute-start(bf16[2,128,1024]{2,1,0:T(8,128)(2,1)S(1)} %get-tuple-element.33.own_ref), channel_id=1, source_target_pairs={{0,1},{1,2},{2,3},{4,5},{5,6},{6,7},{8,9},{9,10},{10,11},{12,13},{... | collective-permute-start | bytes 1572872 | tf_op jit(solution)/shard_map/ppermute | solution.py:188
  29.8 0.8 broadcast_in_dim.38
  30.7 7.6 %all-to-all-start.1 = ((bf16[16,8,2048]{2,1,0:T(8,128)(2,1)}), bf16[16,8,2048]{2,1,0:T(8,128)(2,1)S(1)}, u32[]{:S(2)}, u32[]{:S(2)}) async-start(bf16[16,8,2048]{2,1,0:T(8,128)(2,1)} %broadcast_in_dim.38), calls=%async_computation.1 | async-start | bytes 1048576 | tf_op jit(solution)/shard_map/all_to_all | solution.py:168
  40.9 15.4 %collective-permute-done.2.rest_2_ = bf16[2,128,640]{2,1,0:T(8,128)(2,1)S(1)} collective-permute-done((bf16[2,128,640]{2,1,0:T(8,128)(2,1)S(1)}, bf16[2,128,640]{2,1,0:T(8,128)(2,1)S(1)}, u32[]{:S(2)}, u32[]{:S(2)}) %collective-permute-start.2) | collective-permute-done | bytes 327712 | tf_op jit(solution)/shard_map/ppermute | solution.py:188
  56.3 7.4 %collective-permute-start.4 = (bf16[2,128,640]{2,1,0:T(8,128)(2,1)S(1)}, bf16[2,128,640]{2,1,0:T(8,128)(2,1)S(1)}, u32[]{:S(2)}, u32[]{:S(2)}) collective-permute-start(bf16[2,128,640]{2,1,0:T(8,128)(2,1)S(1)} %collective-permute-done.2.rest_2_), channel_id=1, source_target_pairs={{0,3},{3,2},{4,7},{7,6},{8,11},{11,10},{12,15},{15,14},{16,19},{19... | collective-permute-start | bytes 983048 | tf_op jit(solution)/shard_map/ppermute | solution.py:188
  65.0 1.9 collective-permute-start.3
  66.9 1.2 broadcast_in_dim.40
  68.2 3.3 %all-to-all-start.2 = ((f32[8,1,1]{2,1,0:T(1,128)}), f32[8,1,1]{2,1,0:T(1,128)S(1)}, u32[]{:S(2)}, u32[]{:S(2)}) async-start(f32[8,1,1]{2,1,0:T(1,128)} %broadcast_in_dim.40), calls=%async_computation.2 | async-start | bytes 8192 | tf_op jit(solution)/shard_map/all_to_all | solution.py:168
  72.2 1.3 collective-permute-start.1
  73.5 16.4 %all-to-all-done.2 = f32[8,1,1]{2,1,0:T(1,128)S(1)} async-done(((f32[8,1,1]{2,1,0:T(1,128)}), f32[8,1,1]{2,1,0:T(1,128)S(1)}, u32[]{:S(2)}, u32[]{:S(2)}) %all-to-all-start.2) | async-done | bytes 64 | tf_op jit(solution)/shard_map/all_to_all | solution.py:168
  90.5 1.2 fusion.1
  91.8 4.2 %collective-permute-done.4.rest_1_ = bf16[2,128,640]{2,1,0:T(8,128)(2,1)S(1)} collective-permute-done((bf16[2,128,640]{2,1,0:T(8,128)(2,1)S(1)}, bf16[2,128,640]{2,1,0:T(8,128)(2,1)S(1)}, u32[]{:S(2)}, u32[]{:S(2)}) %collective-permute-start.4) | collective-permute-done | bytes 327712 | tf_op jit(solution)/shard_map/ppermute | solution.py:188
  96.7 1.0 copy-done.9
  97.7 1.0 copy-done.11
  98.6 8.3 %attend.2 = (bf16[1,128,2048]{2,1,0:T(8,128)(2,1)}, bf16[128,1024]{1,0:T(8,128)(2,1)S(1)}, bf16[128,1024]{1,0:T(8,128)(2,1)S(1)}, f32[2,128,640]{2,1,0:T(8,128)S...) custom-call(s32[2]{0:T(128)S(1)} %pad_add_fusion.place_ref, ...), custom_call_target="tpu_custom_call" | custom-call | tf_op jit(solution)/shard_map/attend/pallas_call | solution.py:122
  107.6 1.3 collective-permute-start.8
  108.9 1.3 collective-permute-start.9
  110.2 5.8 %attend.3 = (bf16[1,128,2048]{2,1,0:T(8,128)(2,1)}, bf16[128,1024]{1,0:T(8,128)(2,1)S(1)}, bf16[128,1024]{1,0:T(8,128)(2,1)S(1)}, f32[2,128,384]{2,1,0:T(8,128)S...) custom-call(s32[2]{0:T(128)S(1)} %pad_add_fusion.place_ref, ...), custom_call_target="tpu_custom_call", output_to_operand_aliasing={{0}: (10, {}), {1}: (11, {}), {2}: (12, {})} | custom-call | tf_op jit(solution)/shard_map/attend/pallas_call | solution.py:122
  116.8 1.3 collective-permute-start.7
  118.9 18.6 %collective-permute-done.7.rest_1_ = bf16[2,128,384]{2,1,0:T(8,128)(2,1)S(1)} collective-permute-done((bf16[2,128,384]{2,1,0:T(8,128)(2,1)S(1)}, bf16[2,128,384]{2,1,0:T(8,128)(2,1)S(1)}, u32[]{:S(2)}, u32[]{:S(2)}) %collective-permute-start.7) | collective-permute-done | bytes 196640 | tf_op jit(solution)/shard_map/ppermute | solution.py:188
  138.3 7.5 %all-to-all-start.3 = ((bf16[16,8,2048]{2,1,0:T(8,128)(2,1)}), bf16[16,8,2048]{2,1,0:T(8,128)(2,1)S(1)}, u32[]{:S(2)}, u32[]{:S(2)}) async-start(bf16[16,8,2048]{2,1,0:T(8,128)(2,1)} %maximum_bitcast_fusion), calls=%async_computation.3 | async-start | bytes 1048576 | tf_op jit(solution)/shard_map/all_to_all | solution.py:235
  145.8 1.1 add.13
  146.9 11.9 %collective-permute-start.10 = (bf16[2,128,640]{2,1,0:T(8,128)(2,1)S(1)}, bf16[2,128,640]{2,1,0:T(8,128)(2,1)S(1)}, u32[]{:S(2)}, u32[]{:S(2)}) collective-permute-start(bf16[2,128,640]{2,1,0:T(8,128)(2,1)S(1)} %add.13), channel_id=1, source_target_pairs={{3,0},{0,1},{7,4},{4,5},{11,8},{8,9},{15,12},{12,13},{19,16},{16,1... | collective-permute-start | bytes 983048 | tf_op jit(solution)/shard_map/ppermute | solution.py:188
  158.9 1.4 collective-permute-start.6
  161.0 18.0 %all-to-all-start.4 = ((bf16[4,2,2048]{2,1,0:T(2,128)(2,1)}), bf16[4,2,2048]{2,1,0:T(2,128)(2,1)S(1)}, u32[]{:S(2)}, u32[]{:S(2)}) async-start(bf16[4,2,2048]{2,1,0:T(2,128)(2,1)} %reshape.40), calls=%async_computation.4 | async-start | bytes 65536 | tf_op jit(solution)/shard_map/all_to_all | solution.py:238
  179.0 2.1 %finish.2 = (bf16[1,128,1024]{2,1,0:T(8,128)(2,1)}, bf16[1,128,1024]{2,1,0:T(8,128)(2,1)}) custom-call(f32[2,128,640]{2,1,0:T(8,128)S(1)} %get-tuple-element.46.down_ref, bf16[2,128,640]{2,1,0:T(8,128)(2,1)S(1)} %copy-done.5, bf16[2,128,640]{2,1,0:T(8,128)(2,1)S(1)} %collective-permute-done.10.rest_1_), custom_call_target="tpu_custom_call" | custom-call | tf_op jit(solution)/shard_map/finish/pallas_call | solution.py:151
  181.1 1.4 finish.3
  182.5 9.2 %all-to-all-done.4 = bf16[4,2,2048]{2,1,0:T(2,128)(2,1)S(1)} async-done(((bf16[4,2,2048]{2,1,0:T(2,128)(2,1)}), bf16[4,2,2048]{2,1,0:T(2,128)(2,1)S(1)}, u32[]{:S(2)}, u32[]{:S(2)}) %all-to-all-start.4) | async-done | bytes 32800 | tf_op jit(solution)/shard_map/all_to_all | solution.py:238
  (62 shorter events, 12.1 us)
Async XLA Ops:
  2.0 27.8 %all-to-all-start = ((bf16[4,2,2048]{2,1,0:T(2,128)(2,1)}), bf16[4,2,2048]{2,1,0:T(2,128)(2,1)S(1)}, u32[]{:S(2)}, u32[]{:S(2)}) async-start(bf16[4,2,2048]{2,1,0:T(2,128)(2,1)} %broadcast_in_dim.36), calls=%async_computation | async-start | bytes 65536 | tf_op jit(solution)/shard_map/all_to_all | solution.py:168
  17.1 0.9 copy-start.12
  18.0 0.9 copy-start.13
  19.7 36.6 %collective-permute-start.2 = (bf16[2,128,640]{2,1,0:T(8,128)(2,1)S(1)}, bf16[2,128,640]{2,1,0:T(8,128)(2,1)S(1)}, u32[]{:S(2)}, u32[]{:S(2)}) collective-permute-start(bf16[2,128,640]{2,1,0:T(8,128)(2,1)S(1)} %get-tuple-element.35), channel_id=1, source_target_pairs={{0,3},{1,0},{4,7},{5,4},{8,11},{9,8},{12,15},{13,12},{16,19},{17,1... | collective-permute-start | bytes 983048 | tf_op jit(solution)/shard_map/ppermute | solution.py:188
  27.6 43.9 %collective-permute-start = (bf16[2,128,1024]{2,1,0:T(8,128)(2,1)S(1)}, bf16[2,128,1024]{2,1,0:T(8,128)(2,1)S(1)}, u32[]{:S(2)}, u32[]{:S(2)}) collective-permute-start(bf16[2,128,1024]{2,1,0:T(8,128)(2,1)S(1)} %get-tuple-element.33.own_ref), channel_id=1, source_target_pairs={{0,1},{1,2},{2,3},{4,5},{5,6},{6,7},{8,9},{9,10},{10,11},{12,13},{... | collective-permute-start | bytes 1572872 | tf_op jit(solution)/shard_map/ppermute | solution.py:188
  30.7 66.0 %copy-start = (bf16[1,128,2048]{2,1,0:T(8,128)(2,1)S(1)}, bf16[1,128,2048]{2,1,0:T(8,128)(2,1)}, u32[]{:S(2)}) copy-start(bf16[1,128,2048]{2,1,0:T(8,128)(2,1)} %query_ref.3) | copy-start | bytes 1572868
  30.7 66.0 %copy-start.1 = (bf16[1,128,2048]{2,1,0:T(8,128)(2,1)S(1)}, bf16[1,128,2048]{2,1,0:T(8,128)(2,1)}, u32[]{:S(2)}) copy-start(bf16[1,128,2048]{2,1,0:T(8,128)(2,1)} %grad_ref.3) | copy-start | bytes 1572868
  30.7 36.2 %all-to-all-start.1 = ((bf16[16,8,2048]{2,1,0:T(8,128)(2,1)}), bf16[16,8,2048]{2,1,0:T(8,128)(2,1)S(1)}, u32[]{:S(2)}, u32[]{:S(2)}) async-start(bf16[16,8,2048]{2,1,0:T(8,128)(2,1)} %broadcast_in_dim.38), calls=%async_computation.1 | async-start | bytes 1048576 | tf_op jit(solution)/shard_map/all_to_all | solution.py:168
  56.3 39.7 %copy-start.8 = (bf16[2,128,640]{2,1,0:T(8,128)(2,1)}, bf16[2,128,640]{2,1,0:T(8,128)(2,1)S(1)}, u32[]{:S(2)}) copy-start(bf16[2,128,640]{2,1,0:T(8,128)(2,1)S(1)} %collective-permute-done.2.rest_2_) | copy-start | bytes 983044
  56.3 39.7 %collective-permute-start.4 = (bf16[2,128,640]{2,1,0:T(8,128)(2,1)S(1)}, bf16[2,128,640]{2,1,0:T(8,128)(2,1)S(1)}, u32[]{:S(2)}, u32[]{:S(2)}) collective-permute-start(bf16[2,128,640]{2,1,0:T(8,128)(2,1)S(1)} %collective-permute-done.2.rest_2_), channel_id=1, source_target_pairs={{0,3},{3,2},{4,7},{7,6},{8,11},{11,10},{12,15},{15,14},{16,19},{19... | collective-permute-start | bytes 983048 | tf_op jit(solution)/shard_map/ppermute | solution.py:188
  65.0 45.2 %collective-permute-start.3 = (bf16[2,128,384]{2,1,0:T(8,128)(2,1)}, bf16[2,128,384]{2,1,0:T(8,128)(2,1)S(1)}, u32[]{:S(2)}, u32[]{:S(2)}) collective-permute-start(bf16[2,128,384]{2,1,0:T(8,128)(2,1)} %copy-done.16), channel_id=1, source_target_pairs={{0,3},{4,7},{8,11},{12,15},{16,19},{20,23},{24,27},{28,31},{32,35}... | collective-permute-start | bytes 589832 | tf_op jit(solution)/shard_map/ppermute | solution.py:188
  68.2 21.8 %all-to-all-start.2 = ((f32[8,1,1]{2,1,0:T(1,128)}), f32[8,1,1]{2,1,0:T(1,128)S(1)}, u32[]{:S(2)}, u32[]{:S(2)}) async-start(f32[8,1,1]{2,1,0:T(1,128)} %broadcast_in_dim.40), calls=%async_computation.2 | async-start | bytes 8192 | tf_op jit(solution)/shard_map/all_to_all | solution.py:168
  72.2 38.1 %collective-permute-start.1 = (bf16[2,128,384]{2,1,0:T(8,128)(2,1)}, bf16[2,128,384]{2,1,0:T(8,128)(2,1)}, u32[]{:S(2)}, u32[]{:S(2)}) collective-permute-start(bf16[2,128,384]{2,1,0:T(8,128)(2,1)} %slice.12), channel_id=1, source_target_pairs={{1,2},{2,3},{5,6},{6,7},{9,10},{10,11},{13,14},{14,15},{17,18},{18... | collective-permute-start | bytes 589832 | tf_op jit(solution)/shard_map/ppermute | solution.py:188
  96.0 0.7 copy-start.10
  96.7 1.0 copy-start.9
  97.7 1.0 copy-start.11
  106.9 0.7 copy-start.6
  107.6 29.9 %collective-permute-start.8 = (bf16[2,128,640]{2,1,0:T(8,128)(2,1)S(1)}, bf16[2,128,640]{2,1,0:T(8,128)(2,1)S(1)}, u32[]{:S(2)}, u32[]{:S(2)}) collective-permute-start(bf16[2,128,640]{2,1,0:T(8,128)(2,1)S(1)} %get-tuple-element.47), channel_id=1, source_target_pairs={{3,2},{2,1},{1,0},{7,6},{6,5},{5,4},{11,10},{10,9},{9,8},{15,14},{... | collective-permute-start | bytes 983048 | tf_op jit(solution)/shard_map/ppermute | solution.py:188
  108.9 29.4 %collective-permute-start.9 = (bf16[2,128,640]{2,1,0:T(8,128)(2,1)S(1)}, bf16[2,128,640]{2,1,0:T(8,128)(2,1)}, u32[]{:S(2)}, u32[]{:S(2)}) collective-permute-start(bf16[2,128,640]{2,1,0:T(8,128)(2,1)S(1)} %get-tuple-element.49), channel_id=1, source_target_pairs={{2,3},{3,0},{6,7},{7,4},{10,11},{11,8},{14,15},{15,12},{18,19},{19... | collective-permute-start | bytes 983048 | tf_op jit(solution)/shard_map/ppermute | solution.py:188
  116.1 2.8 %copy-start.2 = (f32[2,128,384]{2,1,0:T(8,128)}, f32[2,128,384]{2,1,0:T(8,128)S(1)}, u32[]{:S(2)}) copy-start(f32[2,128,384]{2,1,0:T(8,128)S(1)} %get-tuple-element.42.down_ref) | copy-start | bytes 1179652
  116.1 2.8 %copy-start.14 = (bf16[2,128,384]{2,1,0:T(8,128)(2,1)}, bf16[2,128,384]{2,1,0:T(8,128)(2,1)S(1)}, u32[]{:S(2)}) copy-start(bf16[2,128,384]{2,1,0:T(8,128)(2,1)S(1)} %get-tuple-element.43) | copy-start | bytes 589828
  116.1 2.8 %collective-permute-start.5 = (bf16[2,128,384]{2,1,0:T(8,128)(2,1)S(1)}, bf16[2,128,384]{2,1,0:T(8,128)(2,1)S(1)}, u32[]{:S(2)}, u32[]{:S(2)}) collective-permute-start(bf16[2,128,384]{2,1,0:T(8,128)(2,1)S(1)} %get-tuple-element.44), channel_id=1, source_target_pairs={{3,2},{2,1},{7,6},{6,5},{11,10},{10,9},{15,14},{14,13},{19,18},{18... | collective-permute-start | bytes 589832 | tf_op jit(solution)/shard_map/ppermute | solution.py:188
  116.8 20.8 %collective-permute-start.7 = (bf16[2,128,384]{2,1,0:T(8,128)(2,1)S(1)}, bf16[2,128,384]{2,1,0:T(8,128)(2,1)S(1)}, u32[]{:S(2)}, u32[]{:S(2)}) collective-permute-start(bf16[2,128,384]{2,1,0:T(8,128)(2,1)S(1)} %get-tuple-element.45), channel_id=1, source_target_pairs={{3,0},{7,4},{11,8},{15,12},{19,16},{23,20},{27,24},{31,28},{35,32}... | collective-permute-start | bytes 589832 | tf_op jit(solution)/shard_map/ppermute | solution.py:188
  118.9 26.9 %copy-start.7 = (bf16[2,128,640]{2,1,0:T(8,128)(2,1)S(1)}, bf16[2,128,640]{2,1,0:T(8,128)(2,1)}, u32[]{:S(2)}) copy-start(bf16[2,128,640]{2,1,0:T(8,128)(2,1)} %copy-done.6) | copy-start | bytes 983044
  137.5 0.7 copy-start.4
  138.3 22.0 %all-to-all-start.3 = ((bf16[16,8,2048]{2,1,0:T(8,128)(2,1)}), bf16[16,8,2048]{2,1,0:T(8,128)(2,1)S(1)}, u32[]{:S(2)}, u32[]{:S(2)}) async-start(bf16[16,8,2048]{2,1,0:T(8,128)(2,1)} %maximum_bitcast_fusion), calls=%async_computation.3 | async-start | bytes 1048576 | tf_op jit(solution)/shard_map/all_to_all | solution.py:235
  145.8 13.0 %copy-start.15 = (bf16[2,128,384]{2,1,0:T(8,128)(2,1)S(1)}, bf16[2,128,384]{2,1,0:T(8,128)(2,1)}, u32[]{:S(2)}) copy-start(bf16[2,128,384]{2,1,0:T(8,128)(2,1)} %copy-done.14) | copy-start | bytes 589828
  146.9 32.1 %collective-permute-start.10 = (bf16[2,128,640]{2,1,0:T(8,128)(2,1)S(1)}, bf16[2,128,640]{2,1,0:T(8,128)(2,1)S(1)}, u32[]{:S(2)}, u32[]{:S(2)}) collective-permute-start(bf16[2,128,640]{2,1,0:T(8,128)(2,1)S(1)} %add.13), channel_id=1, source_target_pairs={{3,0},{0,1},{7,4},{4,5},{11,8},{8,9},{15,12},{12,13},{19,16},{16,1... | collective-permute-start | bytes 983048 | tf_op jit(solution)/shard_map/ppermute | solution.py:188
  158.9 20.2 %copy-start.5 = (bf16[2,128,640]{2,1,0:T(8,128)(2,1)S(1)}, bf16[2,128,640]{2,1,0:T(8,128)(2,1)}, u32[]{:S(2)}) copy-start(bf16[2,128,640]{2,1,0:T(8,128)(2,1)} %copy-done.4) | copy-start | bytes 983044
  158.9 22.2 %collective-permute-start.6 = (bf16[2,128,384]{2,1,0:T(8,128)(2,1)S(1)}, bf16[2,128,384]{2,1,0:T(8,128)(2,1)S(1)}, u32[]{:S(2)}, u32[]{:S(2)}) collective-permute-start(bf16[2,128,384]{2,1,0:T(8,128)(2,1)S(1)} %add.12), channel_id=1, source_target_pairs={{3,2},{2,1},{1,0},{7,6},{6,5},{5,4},{11,10},{10,9},{9,8},{15,14},{... | collective-permute-start | bytes 589832 | tf_op jit(solution)/shard_map/ppermute | solution.py:188
  161.0 30.7 %all-to-all-start.4 = ((bf16[4,2,2048]{2,1,0:T(2,128)(2,1)}), bf16[4,2,2048]{2,1,0:T(2,128)(2,1)S(1)}, u32[]{:S(2)}, u32[]{:S(2)}) async-start(bf16[4,2,2048]{2,1,0:T(2,128)(2,1)} %reshape.40), calls=%async_computation.4 | async-start | bytes 65536 | tf_op jit(solution)/shard_map/all_to_all | solution.py:238
  179.0 2.1 %copy-start.3 = (f32[2,128,384]{2,1,0:T(8,128)S(1)}, f32[2,128,384]{2,1,0:T(8,128)}, u32[]{:S(2)}) copy-start(f32[2,128,384]{2,1,0:T(8,128)} %copy-done.2) | copy-start | bytes 1179652
  (3 other events, 2.0 us)

commit v3 on v2

--- a/solution.py
+++ b/solution.py
@@ -8,7 +8,7 @@
 HEAD_DIM = 128
 RESP_DEVS = 4
 RESP_MAX = 512
-LOW_HEADS = 5
+LOW_HEADS = 4
 
 SCORE_SCALE = 144.0 ** (-0.5)
 LOGIT_CAP = 50.0
@@ -132,26 +132,27 @@
     )(*inputs, *so_far)
 
 
-def finish_kernel(down_ref, *rest):
+def finish_kernel(scale_ref, down_ref, *rest):
     backs = rest[:2]
     dkey_ref, dvalue_ref = rest[-2:]
     for part, out in enumerate((dkey_ref, dvalue_ref)):
         total = down_ref[part]
         for back in backs:
             total = total + back[part].astype(jnp.float32)
-        out[0] = total.astype(out.dtype)
-
-
-def finish_chunk(first, down, back, width, so_far):
+        out[0] = (scale_ref[0] * total).astype(out.dtype)
+
+
+def finish_chunk(first, scale, down, back, width, so_far):
     _, rows, _ = down.shape
     heads = down.shape[2] // HEAD_DIM
     spec = pl.BlockSpec((2, rows, HEAD_DIM), lambda i: (0, 0, i))
     out_spec = pl.BlockSpec((1, rows, HEAD_DIM), lambda i: (0, 0, first + i))
-    inputs = [down, *back]
+    inputs = [scale, down, *back]
     return pl.pallas_call(
         finish_kernel,
         grid=(heads,),
-        in_specs=[spec] * (1 + len(back))
+        in_specs=[pl.BlockSpec(memory_space=pltpu.SMEM)]
+        + [spec] * (1 + len(back))
         + [pl.BlockSpec(memory_space=pl.ANY)] * len(so_far),
         out_specs=[out_spec] * 2,
         out_shape=[jax.ShapeDtypeStruct((1, rows, width), jnp.bfloat16)] * 2,
@@ -191,20 +192,19 @@
     low = own_low.shape[2]
     one = moved(own, (0, 1), (1, 2), (2, 3))
     low_three = moved(own_low, (0, 3), (1, 0))
-    own_high, low_three = lax.optimization_barrier((own_high, low_three))
+    own_high, one = lax.optimization_barrier((own_high, one))
     low_two = moved(low_three, (0, 3), (3, 2))
     high_three = moved(own_high, (0, 3))
     high_two = moved(one[:, :, low:], (1, 2), (2, 3))
 
     prompt_own = jnp.concatenate([prompt_keys[0], prompt_values[0]], axis=1)
-    prompt = spread(prompt_own, "seq", along).reshape(RESP_DEVS * prompt_part, 2 * width)
+    prompt_own, own = lax.optimization_barrier((prompt_own, own))
+    turns = [[(b, (b + d) % RESP_DEVS) for b in range(RESP_DEVS)] for d in (1, 2, 3)]
+    prompt = jnp.concatenate([prompt_own] + [moved(prompt_own, *turn) for turn in turns], axis=0)
+    prompt, low_three = lax.optimization_barrier((prompt, low_three))
     prompt = spread(prompt, "seq", across).reshape(seq_size * prompt_part, 2 * width)
 
-    group_count = jnp.sum(lengths.astype(jnp.float32)).reshape(1, 1)
-    group_count, prompt = lax.optimization_barrier((group_count, prompt))
-    count = jnp.sum(spread(group_count, "group"))
     advantage = rewards[0] - jnp.mean(rewards[0])
-    advantage = advantage * jnp.float32(lax.axis_size("group") * resp_count * RESP_MAX) / count
     chosen = jnp.arange(resp_count, dtype=jnp.int32) == response_id
     weight = jnp.sum(jnp.where(chosen, advantage, jnp.float32(0.0))).reshape(1)
     length = jnp.sum(jnp.where(chosen, lengths[0], 0))
@@ -229,16 +229,30 @@
         (terms, low_one, low_passed, high_passed, high_around)
     )
 
-    done = finish_chunk(0, down_low, (low_one, low_around), width, [])
-    done = finish_chunk(LOW_HEADS, down_high, (high_one, high_around), width, done)
+    group_count = jnp.sum(lengths.astype(jnp.float32)).reshape(1, 1)
+    group_count, low_passed = lax.optimization_barrier((group_count, low_passed))
+    count = jnp.sum(spread(group_count, "group"))
+    scale = (jnp.float32(lax.axis_size("group") * resp_count * RESP_MAX) / count).reshape(1)
+
+    done = finish_chunk(0, scale, down_low, (low_one, low_around), width, [])
+    done = finish_chunk(LOW_HEADS, scale, down_high, (high_one, high_around), width, done)
 
     got = lax.all_to_all(terms, "seq", 0, 0, axis_index_groups=across)
     line_sum = jnp.sum(got.astype(jnp.float32), axis=0)
-    sent = line_sum.astype(jnp.bfloat16).reshape(RESP_DEVS, prompt_part, 2 * width)
+    line_sum = line_sum.astype(jnp.bfloat16).reshape(RESP_DEVS, prompt_part, 2 * width)
+    sent = jnp.stack(
+        [
+            sum(
+                jnp.where((place - b) % RESP_DEVS == d, line_sum[d], jnp.bfloat16(0.0))
+                for d in range(RESP_DEVS)
+            )
+            for b in range(RESP_DEVS)
+        ]
+    )
     got = lax.all_to_all(sent, "seq", 0, 0, axis_index_groups=along)
-    prompt_sum = jnp.sum(got.astype(jnp.float32), axis=0).astype(jnp.bfloat16)
+    prompt_sum = (scale * jnp.sum(got.astype(jnp.float32), axis=0)).astype(jnp.bfloat16)
     return (
-        dquery,
+        (scale * dquery.astype(jnp.float32)).astype(jnp.bfloat16),
         done[0],
         done[1],
         prompt_sum[None, :, :width],

time: 193 us -> 186 us (0.964)
  the two profiles are of different devices: /device:TPU:2 before, /device:TPU:1 now
where the time goes in v3:
time: 186 us; the launch traced here: 184 us
  starting transfers between devices  105 us (56%)
  waiting for transfers between devices  40.2 us (22%)
  Pallas kernels  19.9 us (11%)
  local copies, waits for them, and re-layouts  10.3 us (6%)
  other arithmetic  6.65 us (4%)
  between operations  2.45 us (1%)
    ppermute x14, starting transfers between devices, moved(): return lax.ppermute(value, 'seq', pairs)  50.9 us
    all_to_all x2, starting transfers between devices, spread(): return lax.all_to_all(copies, axis, 0, 0, axis_index_groups=groups)  40.2 us
    ppermute x14, waiting for transfers between devices, moved(): return lax.ppermute(value, 'seq', pairs)  29.7 us
    pallas_call x2, Pallas kernels, attend_chunk(): pl.pallas_call(attend_kernel, grid=(heads,), in_specs=specs + [pl.BlockSp...  14.6 us
    all_to_all x1, starting transfers between devices, body(): got = lax.all_to_all(sent, 'seq', 0, 0, axis_index_groups=along)  7.13 us
    unnamed x40, local copies, waits for them, and re-layouts  6.92 us
    all_to_all x1, starting transfers between devices, body(): got = lax.all_to_all(terms, 'seq', 0, 0, axis_index_groups=across)  6.75 us
    all_to_all x1, waiting for transfers between devices, body(): got = lax.all_to_all(terms, 'seq', 0, 0, axis_index_groups=across)  5.75 us
  transfers between devices with their start and end apart: 18, of which 6 were waited for; matrix products, arithmetic and copies ran while one was open for 5% of the time, Pallas kernels for 10%

profile of v3, /device:TPU:1, one launch (start us, length us, event | category | flops | bytes accessed | tf_op | source)
XLA Modules:
  0.0 184.4 jit_solution(2687885796923243796)
XLA Ops:
  0.6 0.9 copy-done.8
  1.6 0.9 copy-done.9
  3.3 13.4 %collective-permute-start.3 = (bf16[2,128,512]{2,1,0:T(8,128)(2,1)S(1)}, bf16[2,128,512]{2,1,0:T(8,128)(2,1)S(1)}, u32[]{:S(2)}, u32[]{:S(2)}) collective-permute-start(bf16[2,128,512]{2,1,0:T(8,128)(2,1)S(1)} %get-tuple-element.36), channel_id=1, source_target_pairs={{0,3},{1,0},{4,7},{5,4},{8,11},{9,8},{12,15},{13,12},{16,19},{17,1... | collective-permute-start | bytes 786440 | tf_op jit(solution)/shard_map/ppermute | solution.py:189
  16.7 1.3 collective-permute-start.4
  18.1 4.5 %collective-permute-start = (bf16[2,2048]{1,0:T(2,128)(2,1)S(1)}, bf16[2,2048]{1,0:T(2,128)(2,1)S(1)}, u32[]{:S(2)}, u32[]{:S(2)}) collective-permute-start(bf16[2,2048]{1,0:T(2,128)(2,1)S(1)} %pad_maximum_fusion.2), channel_id=1, source_target_pairs={{0,1},{1,2},{2,3},{3,0},{4,5},{5,6},{6,7},{7,4},{8,9},{9,10},{10,1... | collective-permute-start | bytes 24584 | tf_op jit(solution)/shard_map/ppermute | solution.py:189
  22.6 4.4 %collective-permute-start.1 = (bf16[2,2048]{1,0:T(2,128)(2,1)S(1)}, bf16[2,2048]{1,0:T(2,128)(2,1)S(1)}, u32[]{:S(2)}, u32[]{:S(2)}) collective-permute-start(bf16[2,2048]{1,0:T(2,128)(2,1)S(1)} %pad_maximum_fusion.2), channel_id=1, source_target_pairs={{0,2},{1,3},{2,0},{3,1},{4,6},{5,7},{6,4},{7,5},{8,10},{9,11},{10,... | collective-permute-start | bytes 24584 | tf_op jit(solution)/shard_map/ppermute | solution.py:189
  27.0 7.3 %collective-permute-start.2 = (bf16[2,2048]{1,0:T(2,128)(2,1)S(1)}, bf16[2,2048]{1,0:T(2,128)(2,1)S(1)}, u32[]{:S(2)}, u32[]{:S(2)}) collective-permute-start(bf16[2,2048]{1,0:T(2,128)(2,1)S(1)} %pad_maximum_fusion.2), channel_id=1, source_target_pairs={{0,3},{1,0},{2,1},{3,2},{4,7},{5,4},{6,5},{7,6},{8,11},{9,8},{10,9... | collective-permute-start | bytes 24584 | tf_op jit(solution)/shard_map/ppermute | solution.py:189
  34.3 3.9 %collective-permute-done.1 = bf16[2,2048]{1,0:T(2,128)(2,1)S(1)} collective-permute-done((bf16[2,2048]{1,0:T(2,128)(2,1)S(1)}, bf16[2,2048]{1,0:T(2,128)(2,1)S(1)}, u32[]{:S(2)}, u32[]{:S(2)}) %collective-permute-start.1) | collective-permute-done | bytes 8224 | tf_op jit(solution)/shard_map/ppermute | solution.py:189
  38.2 2.3 %collective-permute-done.2 = bf16[2,2048]{1,0:T(2,128)(2,1)S(1)} collective-permute-done((bf16[2,2048]{1,0:T(2,128)(2,1)S(1)}, bf16[2,2048]{1,0:T(2,128)(2,1)S(1)}, u32[]{:S(2)}, u32[]{:S(2)}) %collective-permute-start.2) | collective-permute-done | bytes 8224 | tf_op jit(solution)/shard_map/ppermute | solution.py:189
  41.3 6.9 %all-to-all-start = ((bf16[16,8,2048]{2,1,0:T(8,128)(2,1)}), bf16[16,8,2048]{2,1,0:T(8,128)(2,1)S(1)}, u32[]{:S(2)}, u32[]{:S(2)}) async-start(bf16[16,8,2048]{2,1,0:T(8,128)(2,1)} %broadcast_in_dim.49), calls=%async_computation | async-start | bytes 1048576 | tf_op jit(solution)/shard_map/all_to_all | solution.py:169
  48.3 8.3 %collective-permute-start.5 = (bf16[2,128,512]{2,1,0:T(8,128)(2,1)S(1)}, bf16[2,128,512]{2,1,0:T(8,128)(2,1)S(1)}, u32[]{:S(2)}, u32[]{:S(2)}) collective-permute-start(bf16[2,128,512]{2,1,0:T(8,128)(2,1)S(1)} %collective-permute-done.3.rest_2_), channel_id=1, source_target_pairs={{0,3},{3,2},{4,7},{7,6},{8,11},{11,10},{12,15},{15,14},{16,19},{19... | collective-permute-start | bytes 786440 | tf_op jit(solution)/shard_map/ppermute | solution.py:189
  57.3 1.4 collective-permute-start.7
  58.7 2.5 %collective-permute-start.8 = (bf16[2,128,512]{2,1,0:T(8,128)(2,1)}, bf16[2,128,512]{2,1,0:T(8,128)(2,1)}, u32[]{:S(2)}, u32[]{:S(2)}) collective-permute-start(bf16[2,128,512]{2,1,0:T(8,128)(2,1)} %get-tuple-element.44), channel_id=1, source_target_pairs={{0,3},{4,7},{8,11},{12,15},{16,19},{20,23},{24,27},{28,31},{32,35}... | collective-permute-start | bytes 786440 | tf_op jit(solution)/shard_map/ppermute | solution.py:189
  65.9 0.9 copy-done.11
  66.9 0.9 copy-done.13
  67.8 7.1 %attend.2 = (bf16[1,128,2048]{2,1,0:T(8,128)(2,1)S(1)}, bf16[128,1024]{1,0:T(8,128)(2,1)S(1)}, bf16[128,1024]{1,0:T(8,128)(2,1)S(1)}, f32[2,128,512]{2,1,0:T(8,1...) custom-call(s32[2]{0:T(128)S(1)} %pad_add_fusion.place_ref, ...), custom_call_target="tpu_custom_call" | custom-call | tf_op jit(solution)/shard_map/attend/pallas_call | solution.py:122
  75.8 1.3 collective-permute-start.12
  77.1 1.3 collective-permute-start.6
  78.4 11.6 %collective-permute-done.8.rest_2_ = bf16[2,128,512]{2,1,0:T(8,128)(2,1)} collective-permute-done((bf16[2,128,512]{2,1,0:T(8,128)(2,1)}, bf16[2,128,512]{2,1,0:T(8,128)(2,1)}, u32[]{:S(2)}, u32[]{:S(2)}) %collective-permute-start.8) | collective-permute-done | bytes 262176 | tf_op jit(solution)/shard_map/ppermute | solution.py:189
  90.0 7.5 %attend.3 = (bf16[1,128,2048]{2,1,0:T(8,128)(2,1)S(1)}, bf16[128,1024]{1,0:T(8,128)(2,1)S(1)}, bf16[128,1024]{1,0:T(8,128)(2,1)S(1)}, f32[2,128,512]{2,1,0:T(8,1...) custom-call(s32[2]{0:T(128)S(1)} %pad_add_fusion.place_ref, ...), custom_call_target="tpu_custom_call", output_to_operand_aliasing={{0}: (10, {}), {1}: (11, {}), {2}: (12, {})} | custom-call | tf_op jit(solution)/shard_map/attend/pallas_call | solution.py:122
  97.4 1.3 collective-permute-start.11
  101.5 1.2 broadcast_in_dim.51
  102.7 33.3 %all-to-all-start.1 = ((f32[8,1,1]{2,1,0:T(1,128)}), f32[8,1,1]{2,1,0:T(1,128)S(1)}, u32[]{:S(2)}, u32[]{:S(2)}) async-start(f32[8,1,1]{2,1,0:T(1,128)} %broadcast_in_dim.51), calls=%async_computation.1 | async-start | bytes 8192 | tf_op jit(solution)/shard_map/all_to_all | solution.py:169
  136.0 4.8 %all-to-all-done.1 = f32[8,1,1]{2,1,0:T(1,128)S(1)} async-done(((f32[8,1,1]{2,1,0:T(1,128)}), f32[8,1,1]{2,1,0:T(1,128)S(1)}, u32[]{:S(2)}, u32[]{:S(2)}) %all-to-all-start.1) | async-done | bytes 64 | tf_op jit(solution)/shard_map/all_to_all | solution.py:169
  140.8 6.8 %all-to-all-start.2 = ((bf16[16,8,2048]{2,1,0:T(8,128)(2,1)}), bf16[16,8,2048]{2,1,0:T(8,128)(2,1)S(1)}, u32[]{:S(2)}, u32[]{:S(2)}) async-start(bf16[16,8,2048]{2,1,0:T(8,128)(2,1)} %maximum_bitcast_fusion), calls=%async_computation.2 | async-start | bytes 1048576 | tf_op jit(solution)/shard_map/all_to_all | solution.py:240
  147.8 1.9 %collective-permute-start.13 = (bf16[2,128,512]{2,1,0:T(8,128)(2,1)S(1)}, bf16[2,128,512]{2,1,0:T(8,128)(2,1)S(1)}, u32[]{:S(2)}, u32[]{:S(2)}) collective-permute-start(bf16[2,128,512]{2,1,0:T(8,128)(2,1)S(1)} %add.76), channel_id=1, source_target_pairs={{3,0},{0,1},{7,4},{4,5},{11,8},{8,9},{15,12},{12,13},{19,16},{16,1... | collective-permute-start | bytes 786440 | tf_op jit(solution)/shard_map/ppermute | solution.py:189
  151.1 1.3 collective-permute-start.10
  152.4 5.7 %all-to-all-done.2 = bf16[16,8,2048]{2,1,0:T(8,128)(2,1)S(1)} async-done(((bf16[16,8,2048]{2,1,0:T(8,128)(2,1)}), bf16[16,8,2048]{2,1,0:T(8,128)(2,1)S(1)}, u32[]{:S(2)}, u32[]{:S(2)}) %all-to-all-start.2) | async-done | bytes 524320 | tf_op jit(solution)/shard_map/all_to_all | solution.py:240
  159.0 7.1 %all-to-all-start.3 = ((bf16[4,2,2048]{2,1,0:T(2,128)(2,1)}), bf16[4,2,2048]{2,1,0:T(2,128)(2,1)S(1)}, u32[]{:S(2)}, u32[]{:S(2)}) async-start(bf16[4,2,2048]{2,1,0:T(2,128)(2,1)} %pad_maximum_fusion.1), calls=%async_computation.3 | async-start | bytes 65536 | tf_op jit(solution)/shard_map/all_to_all | solution.py:252
  167.2 3.1 %finish.2 = (bf16[1,128,1024]{2,1,0:T(8,128)(2,1)}, bf16[1,128,1024]{2,1,0:T(8,128)(2,1)}) custom-call(f32[1]{0:T(128)} %bitcast.10.scale_ref, f32[2,128,512]{2,1,0:T(8,128)S(1)} %copy-done.5, bf16[2,128,512]{2,1,0:T(8,128)(2,1)} %collective-permute-done.12.rest_0_, bf16[2,128,512]{2,1,0:T(8,128)(2,1)S(1)} %collective-permute-done.13.rest_1_), custom_call_target="tpu_custom_call" | custom-call | tf_op jit(solution)/shard_map/finish/pallas_call | solution.py:151
  170.3 12.0 %collective-permute-done.10.rest_0_ = bf16[2,128,512]{2,1,0:T(8,128)(2,1)S(1)} collective-permute-done((bf16[2,128,512]{2,1,0:T(8,128)(2,1)S(1)}, bf16[2,128,512]{2,1,0:T(8,128)(2,1)S(1)}, u32[]{:S(2)}, u32[]{:S(2)}) %collective-permute-start.10) | collective-permute-done | bytes 262176 | tf_op jit(solution)/shard_map/ppermute | solution.py:189
  182.3 1.5 finish.3
  (71 shorter events, 13.5 us)
Async XLA Ops:
  0.6 1.0 copy-start.8
  2.5 15.5 %copy-start.17 = (bf16[1,2,1024]{2,1,0:T(2,128)(2,1)S(1)}, bf16[1,2,1024]{2,1,0:T(2,128)(2,1)}, u32[]{:S(2)}) copy-start(bf16[1,2,1024]{2,1,0:T(2,128)(2,1)} %param.12) | copy-start | bytes 12292
  3.3 14.8 %copy-start.16 = (bf16[1,2,1024]{2,1,0:T(2,128)(2,1)S(1)}, bf16[1,2,1024]{2,1,0:T(2,128)(2,1)}, u32[]{:S(2)}) copy-start(bf16[1,2,1024]{2,1,0:T(2,128)(2,1)} %param.13) | copy-start | bytes 12292
  3.3 37.1 %collective-permute-start.3 = (bf16[2,128,512]{2,1,0:T(8,128)(2,1)S(1)}, bf16[2,128,512]{2,1,0:T(8,128)(2,1)S(1)}, u32[]{:S(2)}, u32[]{:S(2)}) collective-permute-start(bf16[2,128,512]{2,1,0:T(8,128)(2,1)S(1)} %get-tuple-element.36), channel_id=1, source_target_pairs={{0,3},{1,0},{4,7},{5,4},{8,11},{9,8},{12,15},{13,12},{16,19},{17,1... | collective-permute-start | bytes 786440 | tf_op jit(solution)/shard_map/ppermute | solution.py:189
  16.7 39.9 %collective-permute-start.4 = (bf16[2,128,1024]{2,1,0:T(8,128)(2,1)S(1)}, bf16[2,128,1024]{2,1,0:T(8,128)(2,1)S(1)}, u32[]{:S(2)}, u32[]{:S(2)}) collective-permute-start(bf16[2,128,1024]{2,1,0:T(8,128)(2,1)S(1)} %get-tuple-element.38.own_ref), channel_id=1, source_target_pairs={{0,1},{1,2},{2,3},{4,5},{5,6},{6,7},{8,9},{9,10},{10,11},{12,13},{... | collective-permute-start | bytes 1572872 | tf_op jit(solution)/shard_map/ppermute | solution.py:189
  18.1 16.2 %collective-permute-start = (bf16[2,2048]{1,0:T(2,128)(2,1)S(1)}, bf16[2,2048]{1,0:T(2,128)(2,1)S(1)}, u32[]{:S(2)}, u32[]{:S(2)}) collective-permute-start(bf16[2,2048]{1,0:T(2,128)(2,1)S(1)} %pad_maximum_fusion.2), channel_id=1, source_target_pairs={{0,1},{1,2},{2,3},{3,0},{4,5},{5,6},{6,7},{7,4},{8,9},{9,10},{10,1... | collective-permute-start | bytes 24584 | tf_op jit(solution)/shard_map/ppermute | solution.py:189
  22.6 15.5 %collective-permute-start.1 = (bf16[2,2048]{1,0:T(2,128)(2,1)S(1)}, bf16[2,2048]{1,0:T(2,128)(2,1)S(1)}, u32[]{:S(2)}, u32[]{:S(2)}) collective-permute-start(bf16[2,2048]{1,0:T(2,128)(2,1)S(1)} %pad_maximum_fusion.2), channel_id=1, source_target_pairs={{0,2},{1,3},{2,0},{3,1},{4,6},{5,7},{6,4},{7,5},{8,10},{9,11},{10,... | collective-permute-start | bytes 24584 | tf_op jit(solution)/shard_map/ppermute | solution.py:189
  27.0 13.4 %collective-permute-start.2 = (bf16[2,2048]{1,0:T(2,128)(2,1)S(1)}, bf16[2,2048]{1,0:T(2,128)(2,1)S(1)}, u32[]{:S(2)}, u32[]{:S(2)}) collective-permute-start(bf16[2,2048]{1,0:T(2,128)(2,1)S(1)} %pad_maximum_fusion.2), channel_id=1, source_target_pairs={{0,3},{1,0},{2,1},{3,2},{4,7},{5,4},{6,5},{7,6},{8,11},{9,8},{10,9... | collective-permute-start | bytes 24584 | tf_op jit(solution)/shard_map/ppermute | solution.py:189
  40.5 7.8 %copy-start.10 = (bf16[2,128,512]{2,1,0:T(8,128)(2,1)}, bf16[2,128,512]{2,1,0:T(8,128)(2,1)S(1)}, u32[]{:S(2)}) copy-start(bf16[2,128,512]{2,1,0:T(8,128)(2,1)S(1)} %collective-permute-done.3.rest_2_) | copy-start | bytes 786436
  41.3 24.6 %copy-start.1 = (bf16[1,128,2048]{2,1,0:T(8,128)(2,1)S(1)}, bf16[1,128,2048]{2,1,0:T(8,128)(2,1)}, u32[]{:S(2)}) copy-start(bf16[1,128,2048]{2,1,0:T(8,128)(2,1)} %grad_ref.3) | copy-start | bytes 1572868
  41.3 24.6 %all-to-all-start = ((bf16[16,8,2048]{2,1,0:T(8,128)(2,1)}), bf16[16,8,2048]{2,1,0:T(8,128)(2,1)S(1)}, u32[]{:S(2)}, u32[]{:S(2)}) async-start(bf16[16,8,2048]{2,1,0:T(8,128)(2,1)} %broadcast_in_dim.49), calls=%async_computation | async-start | bytes 1048576 | tf_op jit(solution)/shard_map/all_to_all | solution.py:169
  48.2 17.7 %copy-start = (bf16[1,128,2048]{2,1,0:T(8,128)(2,1)S(1)}, bf16[1,128,2048]{2,1,0:T(8,128)(2,1)}, u32[]{:S(2)}) copy-start(bf16[1,128,2048]{2,1,0:T(8,128)(2,1)} %query_ref.3) | copy-start | bytes 1572868
  48.3 16.9 %collective-permute-start.5 = (bf16[2,128,512]{2,1,0:T(8,128)(2,1)S(1)}, bf16[2,128,512]{2,1,0:T(8,128)(2,1)S(1)}, u32[]{:S(2)}, u32[]{:S(2)}) collective-permute-start(bf16[2,128,512]{2,1,0:T(8,128)(2,1)S(1)} %collective-permute-done.3.rest_2_), channel_id=1, source_target_pairs={{0,3},{3,2},{4,7},{7,6},{8,11},{11,10},{12,15},{15,14},{16,19},{19... | collective-permute-start | bytes 786440 | tf_op jit(solution)/shard_map/ppermute | solution.py:189
  56.6 4.7 %copy-start.19 = (s32[1,16]{1,0:T(1,128)S(1)}, s32[1,16]{1,0:T(1,128)}, u32[]{:S(2)}) copy-start(s32[1,16]{1,0:T(1,128)} %param.15) | copy-start | bytes 196
  57.3 21.0 %collective-permute-start.7 = (bf16[2,128,512]{2,1,0:T(8,128)(2,1)}, bf16[2,128,512]{2,1,0:T(8,128)(2,1)}, u32[]{:S(2)}, u32[]{:S(2)}) collective-permute-start(bf16[2,128,512]{2,1,0:T(8,128)(2,1)} %slice.18), channel_id=1, source_target_pairs={{1,2},{2,3},{5,6},{6,7},{9,10},{10,11},{13,14},{14,15},{17,18},{18... | collective-permute-start | bytes 786440 | tf_op jit(solution)/shard_map/ppermute | solution.py:189
  58.7 31.3 %collective-permute-start.8 = (bf16[2,128,512]{2,1,0:T(8,128)(2,1)}, bf16[2,128,512]{2,1,0:T(8,128)(2,1)}, u32[]{:S(2)}, u32[]{:S(2)}) collective-permute-start(bf16[2,128,512]{2,1,0:T(8,128)(2,1)} %get-tuple-element.44), channel_id=1, source_target_pairs={{0,3},{4,7},{8,11},{12,15},{16,19},{20,23},{24,27},{28,31},{32,35}... | collective-permute-start | bytes 786440 | tf_op jit(solution)/shard_map/ppermute | solution.py:189
  65.9 1.0 copy-start.11
  75.8 60.2 %collective-permute-start.12 = (bf16[2,128,512]{2,1,0:T(8,128)(2,1)}, bf16[2,128,512]{2,1,0:T(8,128)(2,1)}, u32[]{:S(2)}, u32[]{:S(2)}) collective-permute-start(bf16[2,128,512]{2,1,0:T(8,128)(2,1)} %get-tuple-element.54), channel_id=1, source_target_pairs={{3,2},{2,1},{1,0},{7,6},{6,5},{5,4},{11,10},{10,9},{9,8},{15,14},{... | collective-permute-start | bytes 786440 | tf_op jit(solution)/shard_map/ppermute | solution.py:189
  77.1 23.8 %collective-permute-start.6 = (bf16[2,128,512]{2,1,0:T(8,128)(2,1)S(1)}, bf16[2,128,512]{2,1,0:T(8,128)(2,1)S(1)}, u32[]{:S(2)}, u32[]{:S(2)}) collective-permute-start(bf16[2,128,512]{2,1,0:T(8,128)(2,1)S(1)} %get-tuple-element.42), channel_id=1, source_target_pairs={{2,3},{3,0},{6,7},{7,4},{10,11},{11,8},{14,15},{15,12},{18,19},{19... | collective-permute-start | bytes 786440 | tf_op jit(solution)/shard_map/ppermute | solution.py:189
  97.4 3.4 %copy-start.2 = (f32[2,128,512]{2,1,0:T(8,128)}, f32[2,128,512]{2,1,0:T(8,128)S(1)}, u32[]{:S(2)}) copy-start(f32[2,128,512]{2,1,0:T(8,128)S(1)} %get-tuple-element.49.down_ref) | copy-start | bytes 1572868
  97.4 3.4 %copy-start.6 = (bf16[2,128,512]{2,1,0:T(8,128)(2,1)}, bf16[2,128,512]{2,1,0:T(8,128)(2,1)S(1)}, u32[]{:S(2)}) copy-start(bf16[2,128,512]{2,1,0:T(8,128)(2,1)S(1)} %get-tuple-element.50) | copy-start | bytes 786436
  97.4 38.6 %collective-permute-start.11 = (bf16[2,128,512]{2,1,0:T(8,128)(2,1)}, bf16[2,128,512]{2,1,0:T(8,128)(2,1)S(1)}, u32[]{:S(2)}, u32[]{:S(2)}) collective-permute-start(bf16[2,128,512]{2,1,0:T(8,128)(2,1)} %get-tuple-element.52), channel_id=1, source_target_pairs={{3,0},{7,4},{11,8},{15,12},{19,16},{23,20},{27,24},{31,28},{35,32}... | collective-permute-start | bytes 786440 | tf_op jit(solution)/shard_map/ppermute | solution.py:189
  98.7 37.3 %collective-permute-start.9 = (bf16[2,128,512]{2,1,0:T(8,128)(2,1)}, bf16[2,128,512]{2,1,0:T(8,128)(2,1)S(1)}, u32[]{:S(2)}, u32[]{:S(2)}) collective-permute-start(bf16[2,128,512]{2,1,0:T(8,128)(2,1)} %get-tuple-element.51), channel_id=1, source_target_pairs={{3,2},{2,1},{7,6},{6,5},{11,10},{10,9},{15,14},{14,13},{19,18},{18... | collective-permute-start | bytes 786440 | tf_op jit(solution)/shard_map/ppermute | solution.py:189
  102.7 38.1 %all-to-all-start.1 = ((f32[8,1,1]{2,1,0:T(1,128)}), f32[8,1,1]{2,1,0:T(1,128)S(1)}, u32[]{:S(2)}, u32[]{:S(2)}) async-start(f32[8,1,1]{2,1,0:T(1,128)} %broadcast_in_dim.51), calls=%async_computation.1 | async-start | bytes 8192 | tf_op jit(solution)/shard_map/all_to_all | solution.py:169
  140.8 6.9 %copy-start.15 = (bf16[2,128,512]{2,1,0:T(8,128)(2,1)S(1)}, bf16[2,128,512]{2,1,0:T(8,128)(2,1)}, u32[]{:S(2)}) copy-start(bf16[2,128,512]{2,1,0:T(8,128)(2,1)} %copy-done.14) | copy-start | bytes 786436
  140.8 17.3 %all-to-all-start.2 = ((bf16[16,8,2048]{2,1,0:T(8,128)(2,1)}), bf16[16,8,2048]{2,1,0:T(8,128)(2,1)S(1)}, u32[]{:S(2)}, u32[]{:S(2)}) async-start(bf16[16,8,2048]{2,1,0:T(8,128)(2,1)} %maximum_bitcast_fusion), calls=%async_computation.2 | async-start | bytes 1048576 | tf_op jit(solution)/shard_map/all_to_all | solution.py:240
  147.7 3.3 %copy-start.7 = (bf16[2,128,512]{2,1,0:T(8,128)(2,1)S(1)}, bf16[2,128,512]{2,1,0:T(8,128)(2,1)}, u32[]{:S(2)}) copy-start(bf16[2,128,512]{2,1,0:T(8,128)(2,1)} %copy-done.6) | copy-start | bytes 786436
  147.8 19.3 %collective-permute-start.13 = (bf16[2,128,512]{2,1,0:T(8,128)(2,1)S(1)}, bf16[2,128,512]{2,1,0:T(8,128)(2,1)S(1)}, u32[]{:S(2)}, u32[]{:S(2)}) collective-permute-start(bf16[2,128,512]{2,1,0:T(8,128)(2,1)S(1)} %add.76), channel_id=1, source_target_pairs={{3,0},{0,1},{7,4},{4,5},{11,8},{8,9},{15,12},{12,13},{19,16},{16,1... | collective-permute-start | bytes 786440 | tf_op jit(solution)/shard_map/ppermute | solution.py:189
  151.1 31.2 %collective-permute-start.10 = (bf16[2,128,512]{2,1,0:T(8,128)(2,1)S(1)}, bf16[2,128,512]{2,1,0:T(8,128)(2,1)S(1)}, u32[]{:S(2)}, u32[]{:S(2)}) collective-permute-start(bf16[2,128,512]{2,1,0:T(8,128)(2,1)S(1)} %add.75), channel_id=1, source_target_pairs={{3,2},{2,1},{1,0},{7,6},{6,5},{5,4},{11,10},{10,9},{9,8},{15,14},{... | collective-permute-start | bytes 786440 | tf_op jit(solution)/shard_map/ppermute | solution.py:189
  159.0 24.8 %all-to-all-start.3 = ((bf16[4,2,2048]{2,1,0:T(2,128)(2,1)}), bf16[4,2,2048]{2,1,0:T(2,128)(2,1)S(1)}, u32[]{:S(2)}, u32[]{:S(2)}) async-start(bf16[4,2,2048]{2,1,0:T(2,128)(2,1)} %pad_maximum_fusion.1), calls=%async_computation.3 | async-start | bytes 65536 | tf_op jit(solution)/shard_map/all_to_all | solution.py:252
  166.1 1.1 copy-start.5
  167.2 15.0 %copy-start.3 = (f32[2,128,512]{2,1,0:T(8,128)S(1)}, f32[2,128,512]{2,1,0:T(8,128)}, u32[]{:S(2)}) copy-start(f32[2,128,512]{2,1,0:T(8,128)} %copy-done.2) | copy-start | bytes 1572868
  (6 other events, 4.8 us)

commit v4 on v2

--- a/solution.py
+++ b/solution.py
@@ -8,10 +8,11 @@
 HEAD_DIM = 128
 RESP_DEVS = 4
 RESP_MAX = 512
-LOW_HEADS = 5
+LOW_HEADS = 4
 
 SCORE_SCALE = 144.0 ** (-0.5)
 LOGIT_CAP = 50.0
+COUNT_BASE = 128.0
 VMEM_BYTES = 48 * 1024 * 1024
 PARAMS = dict(compiler_params=pltpu.CompilerParams(vmem_limit_bytes=VMEM_BYTES))
 
@@ -45,7 +46,7 @@
 
 def attend_kernel(place_ref, weight_ref, query_ref, grad_ref, prompt_key_ref, prompt_value_ref, own_ref, *rest):
     fars = rest[: RESP_DEVS - 1]
-    dquery_ref, dprompt_key_ref, dprompt_value_ref, down_ref, *dfars = rest[-(RESP_DEVS + 3) :]
+    dquery_ref, dprompt_ref, down_ref, *dfars = rest[-(RESP_DEVS + 2) :]
     rows = query_ref.shape[1]
     pair = query_ref.shape[2] // HEAD_DIM
     place, length = place_ref[0], place_ref[1]
@@ -82,8 +83,10 @@
         dquery_ref[0, :, c] = dquery[i * rows : (i + 1) * rows]
     dkeys = contract(grad_score, queries, 0, 0)
     dvalues = contract(attn_low, grads, 0, 0)
-    dprompt_key_ref[...] = dkeys[:prompt_rows].astype(dprompt_key_ref.dtype)
-    dprompt_value_ref[...] = dvalues[:prompt_rows].astype(dprompt_value_ref.dtype)
+    wide = dprompt_ref.shape[1] // 2
+    for base, part in ((0, dkeys), (wide, dvalues)):
+        cols = pl.multiple_of(base + pl.program_id(0) * HEAD_DIM, HEAD_DIM)
+        dprompt_ref[:, pl.ds(cols, HEAD_DIM)] = part[:prompt_rows].astype(dprompt_ref.dtype)
     start = prompt_rows
     for out in (down_ref, *dfars):
         stop = start + out.shape[1]
@@ -94,7 +97,7 @@
 
 def attend_chunk(first, heads, where_it_is, weight, queries, grads, prompt, own, far, so_far):
     rows = queries.shape[1]
-    all_heads = prompt.shape[1] // 2 // HEAD_DIM
+    all_heads = (prompt.shape[1] - HEAD_DIM) // 2 // HEAD_DIM
     width = heads * HEAD_DIM
     qcols = queries.shape[2] // all_heads
     smem = pl.BlockSpec(memory_space=pltpu.SMEM)
@@ -112,8 +115,7 @@
     ]
     outs = [
         jax.ShapeDtypeStruct(queries.shape, jnp.bfloat16),
-        jax.ShapeDtypeStruct((prompt.shape[0], all_heads * HEAD_DIM), jnp.bfloat16),
-        jax.ShapeDtypeStruct((prompt.shape[0], all_heads * HEAD_DIM), jnp.bfloat16),
+        jax.ShapeDtypeStruct((prompt.shape[0], 2 * width), jnp.bfloat16),
         jax.ShapeDtypeStruct((2, rows, width), jnp.float32),
     ] + [jax.ShapeDtypeStruct((2, rows, width), jnp.bfloat16) for _ in far]
     inputs = [where_it_is, weight, queries, grads, prompt, prompt, own, *far]
@@ -123,7 +125,7 @@
         attend_kernel,
         grid=(heads,),
         in_specs=specs + [pl.BlockSpec(memory_space=pl.ANY)] * len(so_far),
-        out_specs=[query_spec, key_spec, key_spec] + [own_spec] * RESP_DEVS,
+        out_specs=[query_spec, pl.BlockSpec(outs[1].shape, lambda i: (0, 0))] + [own_spec] * RESP_DEVS,
         out_shape=outs,
         input_output_aliases=aliases,
         cost_estimate=pl.CostEstimate(flops=0, bytes_accessed=0, transcendentals=0),
@@ -191,18 +193,36 @@
     low = own_low.shape[2]
     one = moved(own, (0, 1), (1, 2), (2, 3))
     low_three = moved(own_low, (0, 3), (1, 0))
-    own_high, low_three = lax.optimization_barrier((own_high, low_three))
+    own_high, one = lax.optimization_barrier((own_high, one))
     low_two = moved(low_three, (0, 3), (3, 2))
     high_three = moved(own_high, (0, 3))
     high_two = moved(one[:, :, low:], (1, 2), (2, 3))
 
+    groups = lax.axis_size("group")
+    own_count = jnp.sum(lengths.astype(jnp.float32)).reshape(1, 1)
+    pairs = [
+        (g * seq_size + s, (g + s // RESP_DEVS) % groups * seq_size + s)
+        for g in range(groups)
+        for s in range(seq_size)
+        if s // RESP_DEVS % groups
+    ]
+    other_count = lax.ppermute(own_count, ("group", "seq"), pairs)
+    other_count = jnp.where(response_id % groups == 0, own_count, other_count)
+
     prompt_own = jnp.concatenate([prompt_keys[0], prompt_values[0]], axis=1)
-    prompt = spread(prompt_own, "seq", along).reshape(RESP_DEVS * prompt_part, 2 * width)
-    prompt = spread(prompt, "seq", across).reshape(seq_size * prompt_part, 2 * width)
-
-    group_count = jnp.sum(lengths.astype(jnp.float32)).reshape(1, 1)
-    group_count, prompt = lax.optimization_barrier((group_count, prompt))
-    count = jnp.sum(spread(group_count, "group"))
+    prompt_own, other_count, own = lax.optimization_barrier((prompt_own, other_count, own))
+    turns = [[(b, (b + d) % RESP_DEVS) for b in range(RESP_DEVS)] for d in (1, 2, 3)]
+    prompt = jnp.concatenate([prompt_own] + [moved(prompt_own, *turn) for turn in turns], axis=0)
+    prompt, low_three = lax.optimization_barrier((prompt, low_three))
+    cell = jnp.arange(HEAD_DIM)[None, :]
+    high = jnp.floor(other_count / COUNT_BASE)
+    cells = jnp.where(cell == 0, high, jnp.where(cell == 1, other_count - high * COUNT_BASE, 0.0))
+    cells = jnp.broadcast_to(cells.astype(jnp.bfloat16), (prompt.shape[0], HEAD_DIM))
+    prompt = spread(jnp.concatenate([prompt, cells], axis=1), "seq", across)
+    parts = prompt[:, 0, 2 * width : 2 * width + 2].astype(jnp.float32)
+    prompt = prompt.reshape(seq_size * prompt_part, 2 * width + HEAD_DIM)
+
+    count = jnp.sum(parts[:, 0] * COUNT_BASE + parts[:, 1]) * (groups / resp_all)
     advantage = rewards[0] - jnp.mean(rewards[0])
     advantage = advantage * jnp.float32(lax.axis_size("group") * resp_count * RESP_MAX) / count
     chosen = jnp.arange(resp_count, dtype=jnp.int32) == response_id
@@ -211,30 +231,48 @@
     where_it_is = jnp.stack([place, length]).astype(jnp.int32)
 
     fixed = where_it_is, weight, resp_queries, grad_out, prompt, own
-    *so_far, down_low, b1, b2, b3 = attend_chunk(
+    dquery, terms_low, down_low, b1, b2, b3 = attend_chunk(
         0, LOW_HEADS, *fixed, (one, low_two, low_three), []
     )
     low_passed = moved(b2, (2, 3), (3, 0))
     low_one = moved(b1, (3, 2), (2, 1), (1, 0))
     low_around = moved(b3 + low_passed, (3, 0), (0, 1))
-    *so_far, down_high, b1, b2, b3 = attend_chunk(
-        LOW_HEADS, width // HEAD_DIM - LOW_HEADS, *fixed, (one, high_two, high_three), so_far
+    dquery, terms_high, down_high, b1, b2, b3 = attend_chunk(
+        LOW_HEADS, width // HEAD_DIM - LOW_HEADS, *fixed, (one, high_two, high_three), [dquery]
     )
     high_passed = moved(b2, (3, 2), (2, 1))
     high_around = moved(b3, (3, 0))
     high_one = moved(b1 + high_passed, (3, 2), (2, 1), (1, 0))
-    dquery, *dprompt = so_far
-    terms = jnp.concatenate(dprompt, axis=1).reshape(resp_all, -1, 2 * width)
-    terms, *_ = lax.optimization_barrier(
-        (terms, low_one, low_passed, high_passed, high_around)
-    )
+    low = LOW_HEADS * HEAD_DIM
+    terms_low, terms_high = [
+        terms.reshape(resp_all, -1, terms.shape[1]) for terms in (terms_low, terms_high)
+    ]
+    terms_low, *_ = lax.optimization_barrier((terms_low, low_one, low_passed))
 
     done = finish_chunk(0, down_low, (low_one, low_around), width, [])
     done = finish_chunk(LOW_HEADS, down_high, (high_one, high_around), width, done)
 
-    got = lax.all_to_all(terms, "seq", 0, 0, axis_index_groups=across)
-    line_sum = jnp.sum(got.astype(jnp.float32), axis=0)
-    sent = line_sum.astype(jnp.bfloat16).reshape(RESP_DEVS, prompt_part, 2 * width)
+    line_low, line_high = [
+        jnp.sum(
+            lax.all_to_all(terms, "seq", 0, 0, axis_index_groups=across).astype(jnp.float32), axis=0
+        ).astype(jnp.bfloat16)
+        for terms in (terms_low, terms_high)
+    ]
+    line_low, *_ = lax.optimization_barrier((line_low, high_passed, high_around))
+    line_sum = jnp.concatenate(
+        [line_low[:, :low], line_high[:, : width - low], line_low[:, low:], line_high[:, width - low :]],
+        axis=1,
+    )
+    line_sum = line_sum.reshape(RESP_DEVS, prompt_part, 2 * width)
+    sent = jnp.stack(
+        [
+            sum(
+                jnp.where((place - b) % RESP_DEVS == d, line_sum[d], jnp.bfloat16(0.0))
+                for d in range(RESP_DEVS)
+            )
+            for b in range(RESP_DEVS)
+        ]
+    )
     got = lax.all_to_all(sent, "seq", 0, 0, axis_index_groups=along)
     prompt_sum = jnp.sum(got.astype(jnp.float32), axis=0).astype(jnp.bfloat16)
     return (

time: 193 us -> 195 us (1.010)
  waiting for transfers between devices: 64.2 us -> 33.3 us
  starting transfers between devices: 89.7 us -> 120 us
  between operations: 1.54 us -> 3.73 us
    ppermute x11 -> x14, starting transfers between devices: 38.2 us -> 58.4 us  [moved(): return lax.ppermute(value, 'seq', pairs)]
    all_to_all x1, starting transfers between devices: 18 us -> 37.9 us  [body(): got = lax.all_to_all(sent, 'seq', 0, 0, axis_index_groups=along)]
    ppermute x11 -> x14, waiting for transfers between devices: 38.3 us -> 19.7 us  [moved(): return lax.ppermute(value, 'seq', pairs)]
    all_to_all x3 -> x1, starting transfers between devices: 26 us -> 8.43 us  [spread(): return lax.all_to_all(copies, axis, 0, 0, axis_index_groups=groups)]
    all_to_all x3 -> x1, waiting for transfers between devices: 16.7 us -> 0.01 us  [spread(): return lax.all_to_all(copies, axis, 0, 0, axis_index_groups=groups)]
    all_to_all x1 -> x2, starting transfers between devices: 7.48 us -> 13.4 us  [body(): lax.all_to_all(terms, 'seq', 0, 0, axis_index_groups=across)]
    all_to_all x1 -> x2, waiting for transfers between devices: 0.01 us -> 5.5 us  [body(): lax.all_to_all(terms, 'seq', 0, 0, axis_index_groups=across)]
    unnamed x38 -> x45, local copies, waits for them, and re-layouts: 7.41 us -> 9.53 us
  transfers between devices with their start and end apart: 16 -> 19, of which waited for: 6 -> 5; matrix products, arithmetic and copies ran while one was open for 5% -> 4% of each run, Pallas kernels for 9% -> 10%
where the time goes in v4:
time: 195 us; the launch traced here: 194 us
  starting transfers between devices  120 us (62%)
  waiting for transfers between devices  33.3 us (17%)
  Pallas kernels  18.7 us (10%)
  local copies, waits for them, and re-layouts  11.7 us (6%)
  other arithmetic  6.54 us (3%)
  between operations  3.73 us (2%)
    ppermute x14, starting transfers between devices, moved(): return lax.ppermute(value, 'seq', pairs)  58.4 us
    all_to_all x1, starting transfers between devices, body(): got = lax.all_to_all(sent, 'seq', 0, 0, axis_index_groups=along)  37.9 us
    ppermute x14, waiting for transfers between devices, moved(): return lax.ppermute(value, 'seq', pairs)  19.7 us
    pallas_call x2, Pallas kernels, attend_chunk(): pl.pallas_call(attend_kernel, grid=(heads,), in_specs=specs + [pl.BlockSp...  14.2 us
    all_to_all x2, starting transfers between devices, body(): lax.all_to_all(terms, 'seq', 0, 0, axis_index_groups=across)  13.4 us
    unnamed x45, local copies, waits for them, and re-layouts  9.53 us
    all_to_all x1, starting transfers between devices, spread(): return lax.all_to_all(copies, axis, 0, 0, axis_index_groups=groups)  8.43 us
    all_to_all x1, waiting for transfers between devices, body(): got = lax.all_to_all(sent, 'seq', 0, 0, axis_index_groups=along)  8.16 us
  transfers between devices with their start and end apart: 19, of which 5 were waited for; matrix products, arithmetic and copies ran while one was open for 4% of the time, Pallas kernels for 10%

profile of v4, /device:TPU:2, one launch (start us, length us, event | category | flops | bytes accessed | tf_op | source)
XLA Modules:
  0.0 194.1 jit_solution(4607985748804623591)
XLA Ops:
  0.6 1.3 convert_reduce_fusion
  1.9 1.9 collective-permute-start
  3.8 0.9 copy-done.10
  4.8 0.9 copy-done.11
  6.5 12.7 %collective-permute-start.4 = (bf16[2,128,512]{2,1,0:T(8,128)(2,1)S(1)}, bf16[2,128,512]{2,1,0:T(8,128)(2,1)S(1)}, u32[]{:S(2)}, u32[]{:S(2)}) collective-permute-start(bf16[2,128,512]{2,1,0:T(8,128)(2,1)S(1)} %get-tuple-element.35), channel_id=1, source_target_pairs={{0,3},{1,0},{4,7},{5,4},{8,11},{9,8},{12,15},{13,12},{16,19},{17,1... | collective-permute-start | bytes 786440 | tf_op jit(solution)/shard_map/ppermute | solution.py:190
  19.2 1.3 collective-permute-start.5
  22.6 4.8 %collective-permute-start.1 = (bf16[2,2048]{1,0:T(2,128)(2,1)S(1)}, bf16[2,2048]{1,0:T(2,128)(2,1)S(1)}, u32[]{:S(2)}, u32[]{:S(2)}) collective-permute-start(bf16[2,2048]{1,0:T(2,128)(2,1)S(1)} %pad_maximum_fusion.4), channel_id=1, source_target_pairs={{0,1},{1,2},{2,3},{3,0},{4,5},{5,6},{6,7},{7,4},{8,9},{9,10},{10,1... | collective-permute-start | bytes 24584 | tf_op jit(solution)/shard_map/ppermute | solution.py:190
  27.5 4.4 %collective-permute-start.2 = (bf16[2,2048]{1,0:T(2,128)(2,1)S(1)}, bf16[2,2048]{1,0:T(2,128)(2,1)S(1)}, u32[]{:S(2)}, u32[]{:S(2)}) collective-permute-start(bf16[2,2048]{1,0:T(2,128)(2,1)S(1)} %pad_maximum_fusion.4), channel_id=1, source_target_pairs={{0,2},{1,3},{2,0},{3,1},{4,6},{5,7},{6,4},{7,5},{8,10},{9,11},{10,... | collective-permute-start | bytes 24584 | tf_op jit(solution)/shard_map/ppermute | solution.py:190
  31.8 7.8 %collective-permute-start.3 = (bf16[2,2048]{1,0:T(2,128)(2,1)S(1)}, bf16[2,2048]{1,0:T(2,128)(2,1)S(1)}, u32[]{:S(2)}, u32[]{:S(2)}) collective-permute-start(bf16[2,2048]{1,0:T(2,128)(2,1)S(1)} %pad_maximum_fusion.4), channel_id=1, source_target_pairs={{0,3},{1,0},{2,1},{3,2},{4,7},{5,4},{6,5},{7,6},{8,11},{9,8},{10,9... | collective-permute-start | bytes 24584 | tf_op jit(solution)/shard_map/ppermute | solution.py:190
  39.7 2.8 %collective-permute-done.2 = bf16[2,2048]{1,0:T(2,128)(2,1)S(1)} collective-permute-done((bf16[2,2048]{1,0:T(2,128)(2,1)S(1)}, bf16[2,2048]{1,0:T(2,128)(2,1)S(1)}, u32[]{:S(2)}, u32[]{:S(2)}) %collective-permute-start.2) | collective-permute-done | bytes 8224 | tf_op jit(solution)/shard_map/ppermute | solution.py:190
  42.5 1.4 collective-permute-done.3
  44.8 8.4 %all-to-all-start = ((bf16[16,8,2176]{2,1,0:T(8,128)(2,1)}), bf16[16,8,2176]{2,1,0:T(8,128)(2,1)S(1)}, u32[]{:S(2)}, u32[]{:S(2)}) async-start(bf16[16,8,2176]{2,1,0:T(8,128)(2,1)} %broadcast_in_dim.76), calls=%async_computation | async-start | bytes 1114112 | tf_op jit(solution)/shard_map/all_to_all | solution.py:170
  55.9 7.6 %collective-permute-start.8 = (bf16[2,128,512]{2,1,0:T(8,128)(2,1)S(1)}, bf16[2,128,512]{2,1,0:T(8,128)(2,1)S(1)}, u32[]{:S(2)}, u32[]{:S(2)}) collective-permute-start(bf16[2,128,512]{2,1,0:T(8,128)(2,1)S(1)} %collective-permute-done.4.rest_2_), channel_id=1, source_target_pairs={{0,3},{3,2},{4,7},{7,6},{8,11},{11,10},{12,15},{15,14},{16,19},{19... | collective-permute-start | bytes 786440 | tf_op jit(solution)/shard_map/ppermute | solution.py:190
  65.0 4.7 %collective-permute-start.7 = (bf16[2,128,512]{2,1,0:T(8,128)(2,1)}, bf16[2,128,512]{2,1,0:T(8,128)(2,1)}, u32[]{:S(2)}, u32[]{:S(2)}) collective-permute-start(bf16[2,128,512]{2,1,0:T(8,128)(2,1)} %copy-done.13), channel_id=1, source_target_pairs={{0,3},{4,7},{8,11},{12,15},{16,19},{20,23},{24,27},{28,31},{32,35}... | collective-permute-start | bytes 786440 | tf_op jit(solution)/shard_map/ppermute | solution.py:190
  71.6 15.5 %collective-permute-done.8.rest_1_ = bf16[2,128,512]{2,1,0:T(8,128)(2,1)S(1)} collective-permute-done((bf16[2,128,512]{2,1,0:T(8,128)(2,1)S(1)}, bf16[2,128,512]{2,1,0:T(8,128)(2,1)S(1)}, u32[]{:S(2)}, u32[]{:S(2)}) %collective-permute-start.8) | collective-permute-done | bytes 262176 | tf_op jit(solution)/shard_map/ppermute | solution.py:190
  87.8 0.9 copy-done.9
  88.8 7.0 %attend.2 = (bf16[1,128,2048]{2,1,0:T(8,128)(2,1)}, bf16[128,1024]{1,0:T(8,128)(2,1)}, f32[2,128,512]{2,1,0:T(8,128)S(1)}, bf16[2,128,512]{2,1,0:T(8,128)(2,1)},...) custom-call(s32[2]{0:T(128)S(1)} %pad_add_fusion.place_ref, f32[1]{0:T(128)} %bitcast.12.weight_ref, ...), custom_call_target="tpu_custom_call" | custom-call | tf_op jit(solution)/shard_map/attend/pallas_call | solution.py:124
  95.8 1.3 collective-permute-start.12
  97.0 1.3 collective-permute-start.13
  99.1 0.9 copy-done.7
  100.0 7.2 %attend.3 = (bf16[1,128,2048]{2,1,0:T(8,128)(2,1)}, bf16[128,1024]{1,0:T(8,128)(2,1)S(1)}, f32[2,128,512]{2,1,0:T(8,128)S(1)}, bf16[2,128,512]{2,1,0:T(8,128)(2,...) custom-call(s32[2]{0:T(128)S(1)} %pad_add_fusion.place_ref, ...), custom_call_target="tpu_custom_call", output_to_operand_aliasing={{0}: (10, {})} | custom-call | tf_op jit(solution)/shard_map/attend/pallas_call | solution.py:124
  110.0 8.6 %all-to-all-start.2 = ((bf16[16,8,1024]{2,1,0:T(8,128)(2,1)}), bf16[16,8,1024]{2,1,0:T(8,128)(2,1)S(1)}, u32[]{:S(2)}, u32[]{:S(2)}) async-start(bf16[16,8,1024]{2,1,0:T(8,128)(2,1)} %bitcast.35), calls=%async_computation.2 | async-start | bytes 524288 | tf_op jit(solution)/shard_map/all_to_all | solution.py:257
  119.3 1.3 collective-permute-start.11
  120.6 5.5 %all-to-all-done.2 = bf16[16,8,1024]{2,1,0:T(8,128)(2,1)S(1)} async-done(((bf16[16,8,1024]{2,1,0:T(8,128)(2,1)}), bf16[16,8,1024]{2,1,0:T(8,128)(2,1)S(1)}, u32[]{:S(2)}, u32[]{:S(2)}) %all-to-all-start.2) | async-done | bytes 262176 | tf_op jit(solution)/shard_map/all_to_all | solution.py:257
  126.1 4.8 %all-to-all-start.1 = ((bf16[16,8,1024]{2,1,0:T(8,128)(2,1)}), bf16[16,8,1024]{2,1,0:T(8,128)(2,1)S(1)}, u32[]{:S(2)}, u32[]{:S(2)}) async-start(bf16[16,8,1024]{2,1,0:T(8,128)(2,1)} %bitcast.14), calls=%async_computation.1 | async-start | bytes 524288 | tf_op jit(solution)/shard_map/all_to_all | solution.py:257
  131.0 1.1 add.85
  132.1 8.4 %collective-permute-start.14 = (bf16[2,128,512]{2,1,0:T(8,128)(2,1)S(1)}, bf16[2,128,512]{2,1,0:T(8,128)(2,1)S(1)}, u32[]{:S(2)}, u32[]{:S(2)}) collective-permute-start(bf16[2,128,512]{2,1,0:T(8,128)(2,1)S(1)} %add.85), channel_id=1, source_target_pairs={{3,0},{0,1},{7,4},{4,5},{11,8},{8,9},{15,12},{12,13},{19,16},{16,1... | collective-permute-start | bytes 786440 | tf_op jit(solution)/shard_map/ppermute | solution.py:190
  140.6 1.4 collective-permute-start.10
  142.9 37.9 %all-to-all-start.3 = ((bf16[4,2,2048]{2,1,0:T(2,128)(2,1)}), bf16[4,2,2048]{2,1,0:T(2,128)(2,1)S(1)}, u32[]{:S(2)}, u32[]{:S(2)}) async-start(bf16[4,2,2048]{2,1,0:T(2,128)(2,1)} %pad_maximum_fusion.3), calls=%async_computation.3 | async-start | bytes 65536 | tf_op jit(solution)/shard_map/all_to_all | solution.py:276
  180.8 3.0 %finish.2 = (bf16[1,128,1024]{2,1,0:T(8,128)(2,1)}, bf16[1,128,1024]{2,1,0:T(8,128)(2,1)}) custom-call(f32[2,128,512]{2,1,0:T(8,128)S(1)} %copy-done.3, bf16[2,128,512]{2,1,0:T(8,128)(2,1)} %collective-permute-done.12.rest_0_, bf16[2,128,512]{2,1,0:T(8,128)(2,1)S(1)} %collective-permute-done.14.rest_1_), custom_call_target="tpu_custom_call" | custom-call | tf_op jit(solution)/shard_map/finish/pallas_call | solution.py:153
  183.9 1.5 finish.3
  185.3 8.2 %all-to-all-done.3 = bf16[4,2,2048]{2,1,0:T(2,128)(2,1)S(1)} async-done(((bf16[4,2,2048]{2,1,0:T(2,128)(2,1)}), bf16[4,2,2048]{2,1,0:T(2,128)(2,1)S(1)}, u32[]{:S(2)}, u32[]{:S(2)}) %all-to-all-start.3) | async-done | bytes 32800 | tf_op jit(solution)/shard_map/all_to_all | solution.py:276
  (83 shorter events, 13.6 us)
Async XLA Ops:
  1.9 19.4 %collective-permute-start = (f32[1,1]{1,0:T(1,128)}, f32[1,1]{1,0:T(1,128)}, u32[]{:S(2)}, u32[]{:S(2)}) collective-permute-start(f32[1,1]{1,0:T(1,128)} %bitcast.6), channel_id=1, source_target_pairs={{4,68},{5,69},{6,70},{7,71},{8,136},{9,137},{10,138},{11,139},{12,... | collective-permute-start | bytes 20 | tf_op jit(solution)/shard_map/ppermute | solution.py:209
  3.8 1.0 copy-start.10
  4.8 0.9 copy-start.11
  6.5 37.5 %collective-permute-start.4 = (bf16[2,128,512]{2,1,0:T(8,128)(2,1)S(1)}, bf16[2,128,512]{2,1,0:T(8,128)(2,1)S(1)}, u32[]{:S(2)}, u32[]{:S(2)}) collective-permute-start(bf16[2,128,512]{2,1,0:T(8,128)(2,1)S(1)} %get-tuple-element.35), channel_id=1, source_target_pairs={{0,3},{1,0},{4,7},{5,4},{8,11},{9,8},{12,15},{13,12},{16,19},{17,1... | collective-permute-start | bytes 786440 | tf_op jit(solution)/shard_map/ppermute | solution.py:190
  19.2 44.3 %collective-permute-start.5 = (bf16[2,128,1024]{2,1,0:T(8,128)(2,1)S(1)}, bf16[2,128,1024]{2,1,0:T(8,128)(2,1)S(1)}, u32[]{:S(2)}, u32[]{:S(2)}) collective-permute-start(bf16[2,128,1024]{2,1,0:T(8,128)(2,1)S(1)} %get-tuple-element.38.own_ref), channel_id=1, source_target_pairs={{0,1},{1,2},{2,3},{4,5},{5,6},{6,7},{8,9},{9,10},{10,11},{12,13},{... | collective-permute-start | bytes 1572872 | tf_op jit(solution)/shard_map/ppermute | solution.py:190
  22.6 17.1 %collective-permute-start.1 = (bf16[2,2048]{1,0:T(2,128)(2,1)S(1)}, bf16[2,2048]{1,0:T(2,128)(2,1)S(1)}, u32[]{:S(2)}, u32[]{:S(2)}) collective-permute-start(bf16[2,2048]{1,0:T(2,128)(2,1)S(1)} %pad_maximum_fusion.4), channel_id=1, source_target_pairs={{0,1},{1,2},{2,3},{3,0},{4,5},{5,6},{6,7},{7,4},{8,9},{9,10},{10,1... | collective-permute-start | bytes 24584 | tf_op jit(solution)/shard_map/ppermute | solution.py:190
  27.5 15.0 %collective-permute-start.2 = (bf16[2,2048]{1,0:T(2,128)(2,1)S(1)}, bf16[2,2048]{1,0:T(2,128)(2,1)S(1)}, u32[]{:S(2)}, u32[]{:S(2)}) collective-permute-start(bf16[2,2048]{1,0:T(2,128)(2,1)S(1)} %pad_maximum_fusion.4), channel_id=1, source_target_pairs={{0,2},{1,3},{2,0},{3,1},{4,6},{5,7},{6,4},{7,5},{8,10},{9,11},{10,... | collective-permute-start | bytes 24584 | tf_op jit(solution)/shard_map/ppermute | solution.py:190
  31.8 12.1 %collective-permute-start.3 = (bf16[2,2048]{1,0:T(2,128)(2,1)S(1)}, bf16[2,2048]{1,0:T(2,128)(2,1)S(1)}, u32[]{:S(2)}, u32[]{:S(2)}) collective-permute-start(bf16[2,2048]{1,0:T(2,128)(2,1)S(1)} %pad_maximum_fusion.4), channel_id=1, source_target_pairs={{0,3},{1,0},{2,1},{3,2},{4,7},{5,4},{6,5},{7,6},{8,11},{9,8},{10,9... | collective-permute-start | bytes 24584 | tf_op jit(solution)/shard_map/ppermute | solution.py:190
  44.8 8.5 %copy-start.20 = (f32[1,16]{1,0:T(1,128)S(1)}, f32[1,16]{1,0:T(1,128)}, u32[]{:S(2)}) copy-start(f32[1,16]{1,0:T(1,128)} %param.14) | copy-start | bytes 196
  44.8 9.7 %copy-start.21 = (s32[1,16]{1,0:T(1,128)S(1)}, s32[1,16]{1,0:T(1,128)}, u32[]{:S(2)}) copy-start(s32[1,16]{1,0:T(1,128)} %param.15) | copy-start | bytes 196
  44.8 43.0 %copy-start.1 = (bf16[1,128,2048]{2,1,0:T(8,128)(2,1)S(1)}, bf16[1,128,2048]{2,1,0:T(8,128)(2,1)}, u32[]{:S(2)}) copy-start(bf16[1,128,2048]{2,1,0:T(8,128)(2,1)} %grad_ref.3) | copy-start | bytes 1572868
  44.8 24.8 %all-to-all-start = ((bf16[16,8,2176]{2,1,0:T(8,128)(2,1)}), bf16[16,8,2176]{2,1,0:T(8,128)(2,1)S(1)}, u32[]{:S(2)}, u32[]{:S(2)}) async-start(bf16[16,8,2176]{2,1,0:T(8,128)(2,1)} %broadcast_in_dim.76), calls=%async_computation | async-start | bytes 1114112 | tf_op jit(solution)/shard_map/all_to_all | solution.py:170
  53.3 34.5 %copy-start = (bf16[1,128,2048]{2,1,0:T(8,128)(2,1)S(1)}, bf16[1,128,2048]{2,1,0:T(8,128)(2,1)}, u32[]{:S(2)}) copy-start(bf16[1,128,2048]{2,1,0:T(8,128)(2,1)} %query_ref.3) | copy-start | bytes 1572868
  55.9 31.2 %collective-permute-start.8 = (bf16[2,128,512]{2,1,0:T(8,128)(2,1)S(1)}, bf16[2,128,512]{2,1,0:T(8,128)(2,1)S(1)}, u32[]{:S(2)}, u32[]{:S(2)}) collective-permute-start(bf16[2,128,512]{2,1,0:T(8,128)(2,1)S(1)} %collective-permute-done.4.rest_2_), channel_id=1, source_target_pairs={{0,3},{3,2},{4,7},{7,6},{8,11},{11,10},{12,15},{15,14},{16,19},{19... | collective-permute-start | bytes 786440 | tf_op jit(solution)/shard_map/ppermute | solution.py:190
  64.3 34.1 %collective-permute-start.6 = (bf16[2,128,512]{2,1,0:T(8,128)(2,1)}, bf16[2,128,512]{2,1,0:T(8,128)(2,1)S(1)}, u32[]{:S(2)}, u32[]{:S(2)}) collective-permute-start(bf16[2,128,512]{2,1,0:T(8,128)(2,1)} %slice.61), channel_id=1, source_target_pairs={{1,2},{2,3},{5,6},{6,7},{9,10},{10,11},{13,14},{14,15},{17,18},{18... | collective-permute-start | bytes 786440 | tf_op jit(solution)/shard_map/ppermute | solution.py:190
  65.0 34.1 %collective-permute-start.7 = (bf16[2,128,512]{2,1,0:T(8,128)(2,1)}, bf16[2,128,512]{2,1,0:T(8,128)(2,1)}, u32[]{:S(2)}, u32[]{:S(2)}) collective-permute-start(bf16[2,128,512]{2,1,0:T(8,128)(2,1)} %copy-done.13), channel_id=1, source_target_pairs={{0,3},{4,7},{8,11},{12,15},{16,19},{20,23},{24,27},{28,31},{32,35}... | collective-permute-start | bytes 786440 | tf_op jit(solution)/shard_map/ppermute | solution.py:190
  87.8 1.0 copy-start.9
  95.8 11.4 %copy-start.2 = (f32[2,128,512]{2,1,0:T(8,128)}, f32[2,128,512]{2,1,0:T(8,128)S(1)}, u32[]{:S(2)}) copy-start(f32[2,128,512]{2,1,0:T(8,128)S(1)} %get-tuple-element.49.down_ref) | copy-start | bytes 1572868
  95.8 24.9 %collective-permute-start.12 = (bf16[2,128,512]{2,1,0:T(8,128)(2,1)}, bf16[2,128,512]{2,1,0:T(8,128)(2,1)}, u32[]{:S(2)}, u32[]{:S(2)}) collective-permute-start(bf16[2,128,512]{2,1,0:T(8,128)(2,1)} %get-tuple-element.50), channel_id=1, source_target_pairs={{3,2},{2,1},{1,0},{7,6},{6,5},{5,4},{11,10},{10,9},{9,8},{15,14},{... | collective-permute-start | bytes 786440 | tf_op jit(solution)/shard_map/ppermute | solution.py:190
  97.0 23.6 %collective-permute-start.13 = (bf16[2,128,512]{2,1,0:T(8,128)(2,1)}, bf16[2,128,512]{2,1,0:T(8,128)(2,1)}, u32[]{:S(2)}, u32[]{:S(2)}) collective-permute-start(bf16[2,128,512]{2,1,0:T(8,128)(2,1)} %get-tuple-element.52), channel_id=1, source_target_pairs={{2,3},{3,0},{6,7},{7,4},{10,11},{11,8},{14,15},{15,12},{18,19},{19... | collective-permute-start | bytes 786440 | tf_op jit(solution)/shard_map/ppermute | solution.py:190
  99.1 1.0 copy-start.7
  110.0 8.6 %copy-start.17 = (bf16[2,128,512]{2,1,0:T(8,128)(2,1)S(1)}, bf16[2,128,512]{2,1,0:T(8,128)(2,1)}, u32[]{:S(2)}) copy-start(bf16[2,128,512]{2,1,0:T(8,128)(2,1)} %copy-done.16) | copy-start | bytes 786436
  110.0 9.3 %copy-start.15 = (bf16[2,128,512]{2,1,0:T(8,128)(2,1)S(1)}, bf16[2,128,512]{2,1,0:T(8,128)(2,1)}, u32[]{:S(2)}) copy-start(bf16[2,128,512]{2,1,0:T(8,128)(2,1)} %copy-done.14) | copy-start | bytes 786436
  110.0 16.1 %all-to-all-start.2 = ((bf16[16,8,1024]{2,1,0:T(8,128)(2,1)}), bf16[16,8,1024]{2,1,0:T(8,128)(2,1)S(1)}, u32[]{:S(2)}, u32[]{:S(2)}) async-start(bf16[16,8,1024]{2,1,0:T(8,128)(2,1)} %bitcast.35), calls=%async_computation.2 | async-start | bytes 524288 | tf_op jit(solution)/shard_map/all_to_all | solution.py:257
  118.6 21.9 %collective-permute-start.9 = (bf16[2,128,512]{2,1,0:T(8,128)(2,1)S(1)}, bf16[2,128,512]{2,1,0:T(8,128)(2,1)S(1)}, u32[]{:S(2)}, u32[]{:S(2)}) collective-permute-start(bf16[2,128,512]{2,1,0:T(8,128)(2,1)S(1)} %copy-done.17), channel_id=1, source_target_pairs={{3,2},{2,1},{7,6},{6,5},{11,10},{10,9},{15,14},{14,13},{19,18},{18... | collective-permute-start | bytes 786440 | tf_op jit(solution)/shard_map/ppermute | solution.py:190
  119.3 22.8 %collective-permute-start.11 = (bf16[2,128,512]{2,1,0:T(8,128)(2,1)S(1)}, bf16[2,128,512]{2,1,0:T(8,128)(2,1)S(1)}, u32[]{:S(2)}, u32[]{:S(2)}) collective-permute-start(bf16[2,128,512]{2,1,0:T(8,128)(2,1)S(1)} %copy-done.15), channel_id=1, source_target_pairs={{3,0},{7,4},{11,8},{15,12},{19,16},{23,20},{27,24},{31,28},{35,32}... | collective-permute-start | bytes 786440 | tf_op jit(solution)/shard_map/ppermute | solution.py:190
  126.1 15.9 %all-to-all-start.1 = ((bf16[16,8,1024]{2,1,0:T(8,128)(2,1)}), bf16[16,8,1024]{2,1,0:T(8,128)(2,1)S(1)}, u32[]{:S(2)}, u32[]{:S(2)}) async-start(bf16[16,8,1024]{2,1,0:T(8,128)(2,1)} %bitcast.14), calls=%async_computation.1 | async-start | bytes 524288 | tf_op jit(solution)/shard_map/all_to_all | solution.py:257
  131.0 9.5 %copy-start.5 = (bf16[2,128,512]{2,1,0:T(8,128)(2,1)S(1)}, bf16[2,128,512]{2,1,0:T(8,128)(2,1)}, u32[]{:S(2)}) copy-start(bf16[2,128,512]{2,1,0:T(8,128)(2,1)} %copy-done.4) | copy-start | bytes 786436
  132.1 48.8 %collective-permute-start.14 = (bf16[2,128,512]{2,1,0:T(8,128)(2,1)S(1)}, bf16[2,128,512]{2,1,0:T(8,128)(2,1)S(1)}, u32[]{:S(2)}, u32[]{:S(2)}) collective-permute-start(bf16[2,128,512]{2,1,0:T(8,128)(2,1)S(1)} %add.85), channel_id=1, source_target_pairs={{3,0},{0,1},{7,4},{4,5},{11,8},{8,9},{15,12},{12,13},{19,16},{16,1... | collective-permute-start | bytes 786440 | tf_op jit(solution)/shard_map/ppermute | solution.py:190
  140.5 40.3 %copy-start.3 = (f32[2,128,512]{2,1,0:T(8,128)S(1)}, f32[2,128,512]{2,1,0:T(8,128)}, u32[]{:S(2)}) copy-start(f32[2,128,512]{2,1,0:T(8,128)} %copy-done.2) | copy-start | bytes 1572868
  140.6 43.3 %collective-permute-start.10 = (bf16[2,128,512]{2,1,0:T(8,128)(2,1)S(1)}, bf16[2,128,512]{2,1,0:T(8,128)(2,1)S(1)}, u32[]{:S(2)}, u32[]{:S(2)}) collective-permute-start(bf16[2,128,512]{2,1,0:T(8,128)(2,1)S(1)} %add.84), channel_id=1, source_target_pairs={{3,2},{2,1},{1,0},{7,6},{6,5},{5,4},{11,10},{10,9},{9,8},{15,14},{... | collective-permute-start | bytes 786440 | tf_op jit(solution)/shard_map/ppermute | solution.py:190
  142.9 50.6 %all-to-all-start.3 = ((bf16[4,2,2048]{2,1,0:T(2,128)(2,1)}), bf16[4,2,2048]{2,1,0:T(2,128)(2,1)S(1)}, u32[]{:S(2)}, u32[]{:S(2)}) async-start(bf16[4,2,2048]{2,1,0:T(2,128)(2,1)} %pad_maximum_fusion.3), calls=%async_computation.3 | async-start | bytes 65536 | tf_op jit(solution)/shard_map/all_to_all | solution.py:276
  (9 other events, 6.3 us)

commit v5 on v2

--- a/solution.py
+++ b/solution.py
@@ -8,10 +8,11 @@
 HEAD_DIM = 128
 RESP_DEVS = 4
 RESP_MAX = 512
-LOW_HEADS = 5
+LOW_HEADS = 4
 
 SCORE_SCALE = 144.0 ** (-0.5)
 LOGIT_CAP = 50.0
+COUNT_BASE = 128.0
 VMEM_BYTES = 48 * 1024 * 1024
 PARAMS = dict(compiler_params=pltpu.CompilerParams(vmem_limit_bytes=VMEM_BYTES))
 
@@ -94,7 +95,7 @@
 
 def attend_chunk(first, heads, where_it_is, weight, queries, grads, prompt, own, far, so_far):
     rows = queries.shape[1]
-    all_heads = prompt.shape[1] // 2 // HEAD_DIM
+    all_heads = (prompt.shape[1] - HEAD_DIM) // 2 // HEAD_DIM
     width = heads * HEAD_DIM
     qcols = queries.shape[2] // all_heads
     smem = pl.BlockSpec(memory_space=pltpu.SMEM)
@@ -191,18 +192,36 @@
     low = own_low.shape[2]
     one = moved(own, (0, 1), (1, 2), (2, 3))
     low_three = moved(own_low, (0, 3), (1, 0))
-    own_high, low_three = lax.optimization_barrier((own_high, low_three))
+    own_high, one = lax.optimization_barrier((own_high, one))
     low_two = moved(low_three, (0, 3), (3, 2))
     high_three = moved(own_high, (0, 3))
     high_two = moved(one[:, :, low:], (1, 2), (2, 3))
 
+    groups = lax.axis_size("group")
+    own_count = jnp.sum(lengths.astype(jnp.float32)).reshape(1, 1)
+    pairs = [
+        (g * seq_size + s, (g + s // RESP_DEVS) % groups * seq_size + s)
+        for g in range(groups)
+        for s in range(seq_size)
+        if s // RESP_DEVS % groups
+    ]
+    other_count = lax.ppermute(own_count, ("group", "seq"), pairs)
+    other_count = jnp.where(response_id % groups == 0, own_count, other_count)
+
     prompt_own = jnp.concatenate([prompt_keys[0], prompt_values[0]], axis=1)
-    prompt = spread(prompt_own, "seq", along).reshape(RESP_DEVS * prompt_part, 2 * width)
-    prompt = spread(prompt, "seq", across).reshape(seq_size * prompt_part, 2 * width)
-
-    group_count = jnp.sum(lengths.astype(jnp.float32)).reshape(1, 1)
-    group_count, prompt = lax.optimization_barrier((group_count, prompt))
-    count = jnp.sum(spread(group_count, "group"))
+    prompt_own, other_count, own = lax.optimization_barrier((prompt_own, other_count, own))
+    turns = [[(b, (b + d) % RESP_DEVS) for b in range(RESP_DEVS)] for d in (1, 2, 3)]
+    prompt = jnp.concatenate([prompt_own] + [moved(prompt_own, *turn) for turn in turns], axis=0)
+    prompt, low_three = lax.optimization_barrier((prompt, low_three))
+    cell = jnp.arange(HEAD_DIM)[None, :]
+    high = jnp.floor(other_count / COUNT_BASE)
+    cells = jnp.where(cell == 0, high, jnp.where(cell == 1, other_count - high * COUNT_BASE, 0.0))
+    cells = jnp.broadcast_to(cells.astype(jnp.bfloat16), (prompt.shape[0], HEAD_DIM))
+    prompt = spread(jnp.concatenate([prompt, cells], axis=1), "seq", across)
+    parts = prompt[:, 0, 2 * width : 2 * width + 2].astype(jnp.float32)
+    prompt = prompt.reshape(seq_size * prompt_part, 2 * width + HEAD_DIM)
+
+    count = jnp.sum(parts[:, 0] * COUNT_BASE + parts[:, 1]) * (groups / resp_all)
     advantage = rewards[0] - jnp.mean(rewards[0])
     advantage = advantage * jnp.float32(lax.axis_size("group") * resp_count * RESP_MAX) / count
     chosen = jnp.arange(resp_count, dtype=jnp.int32) == response_id
@@ -234,9 +253,13 @@
 
     got = lax.all_to_all(terms, "seq", 0, 0, axis_index_groups=across)
     line_sum = jnp.sum(got.astype(jnp.float32), axis=0)
-    sent = line_sum.astype(jnp.bfloat16).reshape(RESP_DEVS, prompt_part, 2 * width)
-    got = lax.all_to_all(sent, "seq", 0, 0, axis_index_groups=along)
-    prompt_sum = jnp.sum(got.astype(jnp.float32), axis=0).astype(jnp.bfloat16)
+    line_sum = line_sum.astype(jnp.bfloat16).reshape(RESP_DEVS, prompt_part, 2 * width)
+    parts_back = [
+        moved(line_sum[d], *[(b, (b - d) % RESP_DEVS) for b in range(RESP_DEVS)])
+        for d in range(1, RESP_DEVS)
+    ]
+    prompt_sum = sum(p.astype(jnp.float32) for p in [line_sum[0], *parts_back])
+    prompt_sum = prompt_sum.astype(jnp.bfloat16)
     return (
         dquery,
         done[0],

time: 193 us -> 189 us (0.979)
  the two profiles are of different devices: /device:TPU:2 before, /device:TPU:96 now
where the time goes in v5:
time: 189 us; the launch traced here: 188 us
  starting transfers between devices  81.1 us (43%)
  waiting for transfers between devices  72.8 us (39%)
  Pallas kernels  17.9 us (9%)
  local copies, waits for them, and re-layouts  7.15 us (4%)
  other arithmetic  5.59 us (3%)
  between operations  3.67 us (2%)
    ppermute x17, waiting for transfers between devices, moved(): return lax.ppermute(value, 'seq', pairs)  64.8 us
    ppermute x17, starting transfers between devices, moved(): return lax.ppermute(value, 'seq', pairs)  63 us
    pallas_call x2, Pallas kernels, attend_chunk(): pl.pallas_call(attend_kernel, grid=(heads,), in_specs=specs + [pl.BlockSp...  14.1 us
    all_to_all x1, starting transfers between devices, spread(): return lax.all_to_all(copies, axis, 0, 0, axis_index_groups=groups)  9.32 us
    all_to_all x1, waiting for transfers between devices, body(): got = lax.all_to_all(terms, 'seq', 0, 0, axis_index_groups=across)  8 us
    all_to_all x1, starting transfers between devices, body(): got = lax.all_to_all(terms, 'seq', 0, 0, axis_index_groups=across)  7.58 us
    unnamed x33, local copies, waits for them, and re-layouts  4.92 us
  transfers between devices with their start and end apart: 20, of which 7 were waited for; matrix products, arithmetic and copies ran while one was open for 3% of the time, Pallas kernels for 9%

profile of v5, /device:TPU:96, one launch (start us, length us, event | category | flops | bytes accessed | tf_op | source)
XLA Modules:
  0.0 188.2 jit_solution(13616722124044393998)
XLA Ops:
  0.6 1.3 convert_reduce_fusion
  1.9 1.2 collective-permute-start
  4.1 0.9 copy-done.7
  5.8 10.0 %collective-permute-start.4 = (bf16[2,128,512]{2,1,0:T(8,128)(2,1)S(1)}, bf16[2,128,512]{2,1,0:T(8,128)(2,1)S(1)}, u32[]{:S(2)}, u32[]{:S(2)}) collective-permute-start(bf16[2,128,512]{2,1,0:T(8,128)(2,1)S(1)} %get-tuple-element.36), channel_id=1, source_target_pairs={{0,3},{1,0},{4,7},{5,4},{8,11},{9,8},{12,15},{13,12},{16,19},{17,1... | collective-permute-start | bytes 786440 | tf_op jit(solution)/shard_map/ppermute | solution.py:189
  15.8 1.3 collective-permute-start.5
  19.2 1.9 %collective-permute-start.3 = (bf16[2,2048]{1,0:T(2,128)(2,1)S(1)}, bf16[2,2048]{1,0:T(2,128)(2,1)S(1)}, u32[]{:S(2)}, u32[]{:S(2)}) collective-permute-start(bf16[2,2048]{1,0:T(2,128)(2,1)S(1)} %pad_maximum_fusion.2), channel_id=1, source_target_pairs={{0,3},{1,0},{2,1},{3,2},{4,7},{5,4},{6,5},{7,6},{8,11},{9,8},{10,9... | collective-permute-start | bytes 24584 | tf_op jit(solution)/shard_map/ppermute | solution.py:189
  21.2 10.2 %collective-permute-start.2 = (bf16[2,2048]{1,0:T(2,128)(2,1)S(1)}, bf16[2,2048]{1,0:T(2,128)(2,1)S(1)}, u32[]{:S(2)}, u32[]{:S(2)}) collective-permute-start(bf16[2,2048]{1,0:T(2,128)(2,1)S(1)} %pad_maximum_fusion.2), channel_id=1, source_target_pairs={{0,2},{1,3},{2,0},{3,1},{4,6},{5,7},{6,4},{7,5},{8,10},{9,11},{10,... | collective-permute-start | bytes 24584 | tf_op jit(solution)/shard_map/ppermute | solution.py:189
  31.3 4.9 %collective-permute-start.1 = (bf16[2,2048]{1,0:T(2,128)(2,1)S(1)}, bf16[2,2048]{1,0:T(2,128)(2,1)S(1)}, u32[]{:S(2)}, u32[]{:S(2)}) collective-permute-start(bf16[2,2048]{1,0:T(2,128)(2,1)S(1)} %pad_maximum_fusion.2), channel_id=1, source_target_pairs={{0,1},{1,2},{2,3},{3,0},{4,5},{5,6},{6,7},{7,4},{8,9},{9,10},{10,1... | collective-permute-start | bytes 24584 | tf_op jit(solution)/shard_map/ppermute | solution.py:189
  36.3 27.1 %collective-permute-done.1 = bf16[2,2048]{1,0:T(2,128)(2,1)S(1)} collective-permute-done((bf16[2,2048]{1,0:T(2,128)(2,1)S(1)}, bf16[2,2048]{1,0:T(2,128)(2,1)S(1)}, u32[]{:S(2)}, u32[]{:S(2)}) %collective-permute-start.1) | collective-permute-done | bytes 8224 | tf_op jit(solution)/shard_map/ppermute | solution.py:189
  64.4 9.3 %all-to-all-start = ((bf16[16,8,2176]{2,1,0:T(8,128)(2,1)}), bf16[16,8,2176]{2,1,0:T(8,128)(2,1)S(1)}, u32[]{:S(2)}, u32[]{:S(2)}) async-start(bf16[16,8,2176]{2,1,0:T(8,128)(2,1)} %broadcast_in_dim.57), calls=%async_computation | async-start | bytes 1114112 | tf_op jit(solution)/shard_map/all_to_all | solution.py:169
  76.4 8.3 %collective-permute-start.8 = (bf16[2,128,512]{2,1,0:T(8,128)(2,1)S(1)}, bf16[2,128,512]{2,1,0:T(8,128)(2,1)S(1)}, u32[]{:S(2)}, u32[]{:S(2)}) collective-permute-start(bf16[2,128,512]{2,1,0:T(8,128)(2,1)S(1)} %collective-permute-done.4.rest_2_), channel_id=1, source_target_pairs={{0,3},{3,2},{4,7},{7,6},{8,11},{11,10},{12,15},{15,14},{16,19},{19... | collective-permute-start | bytes 786440 | tf_op jit(solution)/shard_map/ppermute | solution.py:189
  85.4 1.4 collective-permute-start.6
  86.7 5.5 %collective-permute-start.7 = (bf16[2,128,512]{2,1,0:T(8,128)(2,1)}, bf16[2,128,512]{2,1,0:T(8,128)(2,1)}, u32[]{:S(2)}, u32[]{:S(2)}) collective-permute-start(bf16[2,128,512]{2,1,0:T(8,128)(2,1)} %get-tuple-element.42), channel_id=1, source_target_pairs={{0,3},{4,7},{8,11},{12,15},{16,19},{20,23},{24,27},{28,31},{32,35}... | collective-permute-start | bytes 786440 | tf_op jit(solution)/shard_map/ppermute | solution.py:189
  94.2 2.8 %collective-permute-done.8.rest_1_ = bf16[2,128,512]{2,1,0:T(8,128)(2,1)S(1)} collective-permute-done((bf16[2,128,512]{2,1,0:T(8,128)(2,1)S(1)}, bf16[2,128,512]{2,1,0:T(8,128)(2,1)S(1)}, u32[]{:S(2)}, u32[]{:S(2)}) %collective-permute-start.8) | collective-permute-done | bytes 262176 | tf_op jit(solution)/shard_map/ppermute | solution.py:189
  97.0 6.9 %attend.2 = (bf16[1,128,2048]{2,1,0:T(8,128)(2,1)}, bf16[128,1024]{1,0:T(8,128)(2,1)S(1)}, bf16[128,1024]{1,0:T(8,128)(2,1)S(1)}, f32[2,128,512]{2,1,0:T(8,128)S...) custom-call(s32[2]{0:T(128)S(1)} %pad_add_fusion.place_ref, ...), custom_call_target="tpu_custom_call" | custom-call | tf_op jit(solution)/shard_map/attend/pallas_call | solution.py:123
  104.7 1.3 collective-permute-start.12
  106.0 1.3 collective-permute-start.13
  107.3 2.8 %collective-permute-done.7.rest_2_ = bf16[2,128,512]{2,1,0:T(8,128)(2,1)} collective-permute-done((bf16[2,128,512]{2,1,0:T(8,128)(2,1)}, bf16[2,128,512]{2,1,0:T(8,128)(2,1)}, u32[]{:S(2)}, u32[]{:S(2)}) %collective-permute-start.7) | collective-permute-done | bytes 262176 | tf_op jit(solution)/shard_map/ppermute | solution.py:189
  110.1 7.2 %attend.3 = (bf16[1,128,2048]{2,1,0:T(8,128)(2,1)}, bf16[128,1024]{1,0:T(8,128)(2,1)S(1)}, bf16[128,1024]{1,0:T(8,128)(2,1)S(1)}, f32[2,128,512]{2,1,0:T(8,128)S...) custom-call(s32[2]{0:T(128)S(1)} %pad_add_fusion.place_ref, ...), custom_call_target="tpu_custom_call", output_to_operand_aliasing={{0}: (10, {}), {1}: (11, {}), {2}: (12, {})} | custom-call | tf_op jit(solution)/shard_map/attend/pallas_call | solution.py:123
  118.0 1.3 collective-permute-start.11
  120.2 4.8 %collective-permute-done.12.rest_0_ = bf16[2,128,512]{2,1,0:T(8,128)(2,1)S(1)} collective-permute-done((bf16[2,128,512]{2,1,0:T(8,128)(2,1)S(1)}, bf16[2,128,512]{2,1,0:T(8,128)(2,1)S(1)}, u32[]{:S(2)}, u32[]{:S(2)}) %collective-permute-start.12) | collective-permute-done | bytes 262176 | tf_op jit(solution)/shard_map/ppermute | solution.py:189
  126.4 17.9 %collective-permute-done.11.rest_1_ = bf16[2,128,512]{2,1,0:T(8,128)(2,1)S(1)} collective-permute-done((bf16[2,128,512]{2,1,0:T(8,128)(2,1)S(1)}, bf16[2,128,512]{2,1,0:T(8,128)(2,1)S(1)}, u32[]{:S(2)}, u32[]{:S(2)}) %collective-permute-start.11) | collective-permute-done | bytes 262176 | tf_op jit(solution)/shard_map/ppermute | solution.py:189
  144.3 7.6 %all-to-all-start.1 = ((bf16[16,8,2048]{2,1,0:T(8,128)(2,1)}), bf16[16,8,2048]{2,1,0:T(8,128)(2,1)S(1)}, u32[]{:S(2)}, u32[]{:S(2)}) async-start(bf16[16,8,2048]{2,1,0:T(8,128)(2,1)} %maximum_bitcast_fusion), calls=%async_computation.1 | async-start | bytes 1048576 | tf_op jit(solution)/shard_map/all_to_all | solution.py:254
  152.0 1.9 %collective-permute-start.14 = (bf16[2,128,512]{2,1,0:T(8,128)(2,1)S(1)}, bf16[2,128,512]{2,1,0:T(8,128)(2,1)S(1)}, u32[]{:S(2)}, u32[]{:S(2)}) collective-permute-start(bf16[2,128,512]{2,1,0:T(8,128)(2,1)S(1)} %add.31), channel_id=1, source_target_pairs={{3,0},{0,1},{7,4},{4,5},{11,8},{8,9},{15,12},{12,13},{19,16},{16,1... | collective-permute-start | bytes 786440 | tf_op jit(solution)/shard_map/ppermute | solution.py:189
  154.0 1.4 collective-permute-start.10
  155.5 8.0 %all-to-all-done.1 = bf16[16,8,2048]{2,1,0:T(8,128)(2,1)S(1)} async-done(((bf16[16,8,2048]{2,1,0:T(8,128)(2,1)}), bf16[16,8,2048]{2,1,0:T(8,128)(2,1)S(1)}, u32[]{:S(2)}, u32[]{:S(2)}) %all-to-all-start.1) | async-done | bytes 524320 | tf_op jit(solution)/shard_map/all_to_all | solution.py:254
  163.6 1.9 %collective-permute-start.15 = (bf16[2,2048]{1,0:T(2,128)(2,1)S(1)}, bf16[2,2048]{1,0:T(2,128)(2,1)S(1)}, u32[]{:S(2)}, u32[]{:S(2)}) collective-permute-start(bf16[2,2048]{1,0:T(2,128)(2,1)S(1)} %get-tuple-element.63), channel_id=1, source_target_pairs={{0,3},{1,0},{2,1},{3,2},{4,7},{5,4},{6,5},{7,6},{8,11},{9,8},{10,9... | collective-permute-start | bytes 24584 | tf_op jit(solution)/shard_map/ppermute | solution.py:189
  165.5 7.8 %collective-permute-start.17 = (bf16[2,2048]{1,0:T(2,128)(2,1)S(1)}, bf16[2,2048]{1,0:T(2,128)(2,1)S(1)}, u32[]{:S(2)}, u32[]{:S(2)}) collective-permute-start(bf16[2,2048]{1,0:T(2,128)(2,1)S(1)} %get-tuple-element.64), channel_id=1, source_target_pairs={{0,1},{1,2},{2,3},{3,0},{4,5},{5,6},{6,7},{7,4},{8,9},{9,10},{10,1... | collective-permute-start | bytes 24584 | tf_op jit(solution)/shard_map/ppermute | solution.py:189
  173.3 1.9 %collective-permute-start.16 = (bf16[2,2048]{1,0:T(2,128)(2,1)S(1)}, bf16[2,2048]{1,0:T(2,128)(2,1)S(1)}, u32[]{:S(2)}, u32[]{:S(2)}) collective-permute-start(bf16[2,2048]{1,0:T(2,128)(2,1)S(1)} %get-tuple-element.65), channel_id=1, source_target_pairs={{0,2},{1,3},{2,0},{3,1},{4,6},{5,7},{6,4},{7,5},{8,10},{9,11},{10,... | collective-permute-start | bytes 24584 | tf_op jit(solution)/shard_map/ppermute | solution.py:189
  175.3 1.5 finish.2
  176.8 1.5 finish.3
  178.3 9.3 %collective-permute-done.16 = bf16[2,2048]{1,0:T(2,128)(2,1)S(1)} collective-permute-done((bf16[2,2048]{1,0:T(2,128)(2,1)S(1)}, bf16[2,2048]{1,0:T(2,128)(2,1)S(1)}, u32[]{:S(2)}, u32[]{:S(2)}) %collective-permute-start.16) | collective-permute-done | bytes 8224 | tf_op jit(solution)/shard_map/ppermute | solution.py:189
  (68 shorter events, 12.0 us)
Async XLA Ops:
  1.9 16.0 %collective-permute-start = (f32[1,1]{1,0:T(1,128)}, f32[1,1]{1,0:T(1,128)}, u32[]{:S(2)}, u32[]{:S(2)}) collective-permute-start(f32[1,1]{1,0:T(1,128)} %bitcast.6), channel_id=1, source_target_pairs={{4,68},{5,69},{6,70},{7,71},{8,136},{9,137},{10,138},{11,139},{12,... | collective-permute-start | bytes 20 | tf_op jit(solution)/shard_map/ppermute | solution.py:208
  3.1 0.9 copy-start.6
  4.1 0.9 copy-start.7
  5.8 57.7 %collective-permute-start.4 = (bf16[2,128,512]{2,1,0:T(8,128)(2,1)S(1)}, bf16[2,128,512]{2,1,0:T(8,128)(2,1)S(1)}, u32[]{:S(2)}, u32[]{:S(2)}) collective-permute-start(bf16[2,128,512]{2,1,0:T(8,128)(2,1)S(1)} %get-tuple-element.36), channel_id=1, source_target_pairs={{0,3},{1,0},{4,7},{5,4},{8,11},{9,8},{12,15},{13,12},{16,19},{17,1... | collective-permute-start | bytes 786440 | tf_op jit(solution)/shard_map/ppermute | solution.py:189
  15.8 68.8 %collective-permute-start.5 = (bf16[2,128,1024]{2,1,0:T(8,128)(2,1)S(1)}, bf16[2,128,1024]{2,1,0:T(8,128)(2,1)S(1)}, u32[]{:S(2)}, u32[]{:S(2)}) collective-permute-start(bf16[2,128,1024]{2,1,0:T(8,128)(2,1)S(1)} %get-tuple-element.39.own_ref), channel_id=1, source_target_pairs={{0,1},{1,2},{2,3},{4,5},{5,6},{6,7},{8,9},{9,10},{10,11},{12,13},{... | collective-permute-start | bytes 1572872 | tf_op jit(solution)/shard_map/ppermute | solution.py:189
  19.2 17.1 %collective-permute-start.3 = (bf16[2,2048]{1,0:T(2,128)(2,1)S(1)}, bf16[2,2048]{1,0:T(2,128)(2,1)S(1)}, u32[]{:S(2)}, u32[]{:S(2)}) collective-permute-start(bf16[2,2048]{1,0:T(2,128)(2,1)S(1)} %pad_maximum_fusion.2), channel_id=1, source_target_pairs={{0,3},{1,0},{2,1},{3,2},{4,7},{5,4},{6,5},{7,6},{8,11},{9,8},{10,9... | collective-permute-start | bytes 24584 | tf_op jit(solution)/shard_map/ppermute | solution.py:189
  21.2 15.1 %collective-permute-start.2 = (bf16[2,2048]{1,0:T(2,128)(2,1)S(1)}, bf16[2,2048]{1,0:T(2,128)(2,1)S(1)}, u32[]{:S(2)}, u32[]{:S(2)}) collective-permute-start(bf16[2,2048]{1,0:T(2,128)(2,1)S(1)} %pad_maximum_fusion.2), channel_id=1, source_target_pairs={{0,2},{1,3},{2,0},{3,1},{4,6},{5,7},{6,4},{7,5},{8,10},{9,11},{10,... | collective-permute-start | bytes 24584 | tf_op jit(solution)/shard_map/ppermute | solution.py:189
  31.3 32.1 %collective-permute-start.1 = (bf16[2,2048]{1,0:T(2,128)(2,1)S(1)}, bf16[2,2048]{1,0:T(2,128)(2,1)S(1)}, u32[]{:S(2)}, u32[]{:S(2)}) collective-permute-start(bf16[2,2048]{1,0:T(2,128)(2,1)S(1)} %pad_maximum_fusion.2), channel_id=1, source_target_pairs={{0,1},{1,2},{2,3},{3,0},{4,5},{5,6},{6,7},{7,4},{8,9},{9,10},{10,1... | collective-permute-start | bytes 24584 | tf_op jit(solution)/shard_map/ppermute | solution.py:189
  64.4 9.4 %copy-start.14 = (f32[1,16]{1,0:T(1,128)S(1)}, f32[1,16]{1,0:T(1,128)}, u32[]{:S(2)}) copy-start(f32[1,16]{1,0:T(1,128)} %param.14) | copy-start | bytes 196
  64.4 10.6 %copy-start.15 = (s32[1,16]{1,0:T(1,128)S(1)}, s32[1,16]{1,0:T(1,128)}, u32[]{:S(2)}) copy-start(s32[1,16]{1,0:T(1,128)} %param.15) | copy-start | bytes 196
  64.4 32.6 %copy-start.1 = (bf16[1,128,2048]{2,1,0:T(8,128)(2,1)S(1)}, bf16[1,128,2048]{2,1,0:T(8,128)(2,1)}, u32[]{:S(2)}) copy-start(bf16[1,128,2048]{2,1,0:T(8,128)(2,1)} %grad_ref.3) | copy-start | bytes 1572868
  64.4 27.8 %all-to-all-start = ((bf16[16,8,2176]{2,1,0:T(8,128)(2,1)}), bf16[16,8,2176]{2,1,0:T(8,128)(2,1)S(1)}, u32[]{:S(2)}, u32[]{:S(2)}) async-start(bf16[16,8,2176]{2,1,0:T(8,128)(2,1)} %broadcast_in_dim.57), calls=%async_computation | async-start | bytes 1114112 | tf_op jit(solution)/shard_map/all_to_all | solution.py:169
  73.7 23.3 %copy-start = (bf16[1,128,2048]{2,1,0:T(8,128)(2,1)S(1)}, bf16[1,128,2048]{2,1,0:T(8,128)(2,1)}, u32[]{:S(2)}) copy-start(bf16[1,128,2048]{2,1,0:T(8,128)(2,1)} %query_ref.3) | copy-start | bytes 1572868
  76.4 20.6 %collective-permute-start.8 = (bf16[2,128,512]{2,1,0:T(8,128)(2,1)S(1)}, bf16[2,128,512]{2,1,0:T(8,128)(2,1)S(1)}, u32[]{:S(2)}, u32[]{:S(2)}) collective-permute-start(bf16[2,128,512]{2,1,0:T(8,128)(2,1)S(1)} %collective-permute-done.4.rest_2_), channel_id=1, source_target_pairs={{0,3},{3,2},{4,7},{7,6},{8,11},{11,10},{12,15},{15,14},{16,19},{19... | collective-permute-start | bytes 786440 | tf_op jit(solution)/shard_map/ppermute | solution.py:189
  85.4 21.9 %collective-permute-start.6 = (bf16[2,128,512]{2,1,0:T(8,128)(2,1)}, bf16[2,128,512]{2,1,0:T(8,128)(2,1)}, u32[]{:S(2)}, u32[]{:S(2)}) collective-permute-start(bf16[2,128,512]{2,1,0:T(8,128)(2,1)} %slice.37), channel_id=1, source_target_pairs={{1,2},{2,3},{5,6},{6,7},{9,10},{10,11},{13,14},{14,15},{17,18},{18... | collective-permute-start | bytes 786440 | tf_op jit(solution)/shard_map/ppermute | solution.py:189
  86.7 23.4 %collective-permute-start.7 = (bf16[2,128,512]{2,1,0:T(8,128)(2,1)}, bf16[2,128,512]{2,1,0:T(8,128)(2,1)}, u32[]{:S(2)}, u32[]{:S(2)}) collective-permute-start(bf16[2,128,512]{2,1,0:T(8,128)(2,1)} %get-tuple-element.42), channel_id=1, source_target_pairs={{0,3},{4,7},{8,11},{12,15},{16,19},{20,23},{24,27},{28,31},{32,35}... | collective-permute-start | bytes 786440 | tf_op jit(solution)/shard_map/ppermute | solution.py:189
  103.9 0.8 copy-start.2
  104.7 20.3 %collective-permute-start.12 = (bf16[2,128,512]{2,1,0:T(8,128)(2,1)S(1)}, bf16[2,128,512]{2,1,0:T(8,128)(2,1)S(1)}, u32[]{:S(2)}, u32[]{:S(2)}) collective-permute-start(bf16[2,128,512]{2,1,0:T(8,128)(2,1)S(1)} %get-tuple-element.53), channel_id=1, source_target_pairs={{3,2},{2,1},{1,0},{7,6},{6,5},{5,4},{11,10},{10,9},{9,8},{15,14},{... | collective-permute-start | bytes 786440 | tf_op jit(solution)/shard_map/ppermute | solution.py:189
  106.0 19.7 %collective-permute-start.13 = (bf16[2,128,512]{2,1,0:T(8,128)(2,1)S(1)}, bf16[2,128,512]{2,1,0:T(8,128)(2,1)S(1)}, u32[]{:S(2)}, u32[]{:S(2)}) collective-permute-start(bf16[2,128,512]{2,1,0:T(8,128)(2,1)S(1)} %get-tuple-element.55), channel_id=1, source_target_pairs={{2,3},{3,0},{6,7},{7,4},{10,11},{11,8},{14,15},{15,12},{18,19},{19... | collective-permute-start | bytes 786440 | tf_op jit(solution)/shard_map/ppermute | solution.py:189
  117.4 2.8 %copy-start.4 = (bf16[2,128,512]{2,1,0:T(8,128)(2,1)}, bf16[2,128,512]{2,1,0:T(8,128)(2,1)S(1)}, u32[]{:S(2)}) copy-start(bf16[2,128,512]{2,1,0:T(8,128)(2,1)S(1)} %get-tuple-element.49) | copy-start | bytes 786436
  117.4 8.3 %collective-permute-start.9 = (bf16[2,128,512]{2,1,0:T(8,128)(2,1)S(1)}, bf16[2,128,512]{2,1,0:T(8,128)(2,1)S(1)}, u32[]{:S(2)}, u32[]{:S(2)}) collective-permute-start(bf16[2,128,512]{2,1,0:T(8,128)(2,1)S(1)} %get-tuple-element.50), channel_id=1, source_target_pairs={{3,2},{2,1},{7,6},{6,5},{11,10},{10,9},{15,14},{14,13},{19,18},{18... | collective-permute-start | bytes 786440 | tf_op jit(solution)/shard_map/ppermute | solution.py:189
  118.0 26.3 %collective-permute-start.11 = (bf16[2,128,512]{2,1,0:T(8,128)(2,1)S(1)}, bf16[2,128,512]{2,1,0:T(8,128)(2,1)S(1)}, u32[]{:S(2)}, u32[]{:S(2)}) collective-permute-start(bf16[2,128,512]{2,1,0:T(8,128)(2,1)S(1)} %get-tuple-element.51), channel_id=1, source_target_pairs={{3,0},{7,4},{11,8},{15,12},{19,16},{23,20},{27,24},{31,28},{35,32}... | collective-permute-start | bytes 786440 | tf_op jit(solution)/shard_map/ppermute | solution.py:189
  144.3 7.6 %copy-start.11 = (bf16[2,128,512]{2,1,0:T(8,128)(2,1)S(1)}, bf16[2,128,512]{2,1,0:T(8,128)(2,1)}, u32[]{:S(2)}) copy-start(bf16[2,128,512]{2,1,0:T(8,128)(2,1)} %copy-done.10) | copy-start | bytes 786436
  144.3 19.1 %all-to-all-start.1 = ((bf16[16,8,2048]{2,1,0:T(8,128)(2,1)}), bf16[16,8,2048]{2,1,0:T(8,128)(2,1)S(1)}, u32[]{:S(2)}, u32[]{:S(2)}) async-start(bf16[16,8,2048]{2,1,0:T(8,128)(2,1)} %maximum_bitcast_fusion), calls=%async_computation.1 | async-start | bytes 1048576 | tf_op jit(solution)/shard_map/all_to_all | solution.py:254
  151.9 2.0 %copy-start.5 = (bf16[2,128,512]{2,1,0:T(8,128)(2,1)S(1)}, bf16[2,128,512]{2,1,0:T(8,128)(2,1)}, u32[]{:S(2)}) copy-start(bf16[2,128,512]{2,1,0:T(8,128)(2,1)} %copy-done.4) | copy-start | bytes 786436
  152.0 23.3 %collective-permute-start.14 = (bf16[2,128,512]{2,1,0:T(8,128)(2,1)S(1)}, bf16[2,128,512]{2,1,0:T(8,128)(2,1)S(1)}, u32[]{:S(2)}, u32[]{:S(2)}) collective-permute-start(bf16[2,128,512]{2,1,0:T(8,128)(2,1)S(1)} %add.31), channel_id=1, source_target_pairs={{3,0},{0,1},{7,4},{4,5},{11,8},{8,9},{15,12},{12,13},{19,16},{16,1... | collective-permute-start | bytes 786440 | tf_op jit(solution)/shard_map/ppermute | solution.py:189
  153.9 21.3 %copy-start.3 = (f32[2,128,512]{2,1,0:T(8,128)S(1)}, f32[2,128,512]{2,1,0:T(8,128)}, u32[]{:S(2)}) copy-start(f32[2,128,512]{2,1,0:T(8,128)} %copy-done.2) | copy-start | bytes 1572868
  154.0 21.3 %copy-start.9 = (bf16[2,128,512]{2,1,0:T(8,128)(2,1)S(1)}, bf16[2,128,512]{2,1,0:T(8,128)(2,1)}, u32[]{:S(2)}) copy-start(bf16[2,128,512]{2,1,0:T(8,128)(2,1)} %copy-done.8) | copy-start | bytes 786436
  154.0 22.8 %collective-permute-start.10 = (bf16[2,128,512]{2,1,0:T(8,128)(2,1)S(1)}, bf16[2,128,512]{2,1,0:T(8,128)(2,1)S(1)}, u32[]{:S(2)}, u32[]{:S(2)}) collective-permute-start(bf16[2,128,512]{2,1,0:T(8,128)(2,1)S(1)} %add.30), channel_id=1, source_target_pairs={{3,2},{2,1},{1,0},{7,6},{6,5},{5,4},{11,10},{10,9},{9,8},{15,14},{... | collective-permute-start | bytes 786440 | tf_op jit(solution)/shard_map/ppermute | solution.py:189
  163.6 14.7 %collective-permute-start.15 = (bf16[2,2048]{1,0:T(2,128)(2,1)S(1)}, bf16[2,2048]{1,0:T(2,128)(2,1)S(1)}, u32[]{:S(2)}, u32[]{:S(2)}) collective-permute-start(bf16[2,2048]{1,0:T(2,128)(2,1)S(1)} %get-tuple-element.63), channel_id=1, source_target_pairs={{0,3},{1,0},{2,1},{3,2},{4,7},{5,4},{6,5},{7,6},{8,11},{9,8},{10,9... | collective-permute-start | bytes 24584 | tf_op jit(solution)/shard_map/ppermute | solution.py:189
  165.5 12.8 %collective-permute-start.17 = (bf16[2,2048]{1,0:T(2,128)(2,1)S(1)}, bf16[2,2048]{1,0:T(2,128)(2,1)S(1)}, u32[]{:S(2)}, u32[]{:S(2)}) collective-permute-start(bf16[2,2048]{1,0:T(2,128)(2,1)S(1)} %get-tuple-element.64), channel_id=1, source_target_pairs={{0,1},{1,2},{2,3},{3,0},{4,5},{5,6},{6,7},{7,4},{8,9},{9,10},{10,1... | collective-permute-start | bytes 24584 | tf_op jit(solution)/shard_map/ppermute | solution.py:189
  173.3 14.3 %collective-permute-start.16 = (bf16[2,2048]{1,0:T(2,128)(2,1)S(1)}, bf16[2,2048]{1,0:T(2,128)(2,1)S(1)}, u32[]{:S(2)}, u32[]{:S(2)}) collective-permute-start(bf16[2,2048]{1,0:T(2,128)(2,1)S(1)} %get-tuple-element.65), channel_id=1, source_target_pairs={{0,2},{1,3},{2,0},{3,1},{4,6},{5,7},{6,4},{7,5},{8,10},{9,11},{10,... | collective-permute-start | bytes 24584 | tf_op jit(solution)/shard_map/ppermute | solution.py:189
  (4 other events, 2.8 us)
